TPU v7x, 32 devices: a whole 2x2x4 slice. The times are simulated.
32 devices in a mesh: row: 8 (over y, x, core), col: 4 (over z).
Axes of the slice: x: 2, y: 2, z: 4, core: 2. Of those that a mesh axis runs over, the one named last changes fastest.
Arguments:
- window: float32 [8, 8192, 4, 1024], P('row', None, 'col'), may hold values from -7 to 8, as said below
Outputs:
- factored: float32 [8, 8192, 4, 1024], P('row', None, 'col')
Inputs may be any that keep to these rules, and one draw needn't show every extreme that they name: `window`: entries above the diagonal are never read. The leading 2 * 128 by 256 block (lower triangle mirrored) is positive definite, with smallest eigenvalue 1 or more.
All inputs are finite; a program needn't handle non-finite values.
Results may differ from a plain program's by a relative error of at most 0.00028.
Values sent between devices are 32-bit elements; how exact they have to be, the bound alone decides.
No kernel may reach another device: no remote copies, remote signals or barrier semaphores. Data moves between devices by JAX's collectives and lax.ppermute only.
A program may use at most 192 MiB of HBM per device.

v0:
```python
import functools

import jax
import jax.numpy as jnp
from jax import lax
from jax.experimental import pallas as pl
from jax.experimental.pallas import tpu as pltpu
from jax.sharding import PartitionSpec as P

NB = 128
KW = 2 * NB
LANES = 128
BLOCK = 32
TILE = 512
F32 = jnp.float32
BF16 = jnp.bfloat16
HI = lax.Precision.HIGHEST
PARAMS = pltpu.CompilerParams(vmem_limit_bytes=48 * 1024 * 1024)


def iota(shape, dim):
    return lax.broadcasted_iota(jnp.int32, shape, dim)


def split(x):
    high = x.astype(BF16)
    return high, (x - high.astype(F32)).astype(BF16)


def dot3(a, b_high, b_low):
    a_high, a_low = split(a)
    dot = functools.partial(jnp.dot, preferred_element_type=F32)
    return dot(a_high, b_high) + (dot(a_high, b_low) + dot(a_low, b_high))


def pack_kernel(width, win_ref, out_ref):
    fold = LANES // width
    part = win_ref.shape[0] // fold
    tile = win_ref[:, 0, :]
    lane = iota((part, LANES), 1) // width
    out = tile[:part]
    for j in range(1, fold):
        rolled = pltpu.roll(tile[j * part : (j + 1) * part], j * width, 1)
        out = jnp.where(lane == j, rolled, out)
    out_ref[...] = out


def pack_rows(window, first, rows, tile, width):
    fold = LANES // width
    base = first // tile
    return pl.pallas_call(
        functools.partial(pack_kernel, width),
        grid=(rows // tile,),
        in_specs=[pl.BlockSpec((None, tile, 1, LANES), lambda i: (0, base + i, 0, 0))],
        out_specs=pl.BlockSpec((tile // fold, LANES), lambda i: (i, 0)),
        out_shape=jax.ShapeDtypeStruct((rows // fold, LANES), F32),
        compiler_params=PARAMS,
        name="pack",
    )(window)


def unpack(slots, width):
    fold = LANES // width
    part = slots[0].shape[0]
    lane = iota((part, LANES), 1) // width
    rows = []
    for j in range(fold):
        pieces = []
        for v in range(len(slots) // fold):
            piece = None
            for m in range(fold):
                slot = slots[v * fold + m]
                shift = (m - j) % fold
                moved = pltpu.roll(slot, shift * width, 1) if shift else slot
                piece = moved if piece is None else jnp.where(lane == m, moved, piece)
            pieces.append(piece)
        rows.append(jnp.concatenate(pieces, 1))
    return jnp.concatenate(rows, 0)


def slot_place(count, width, col_index):
    a = iota((KW, KW), 0)
    c = iota((KW, KW), 1)
    source = lax.rem(col_index - a // width + count, count)
    return (c == lax.rem(a, width) * count + source).astype(F32)


def interleave(ref, first, step, rows):
    for v in range(ref.shape[0]):
        piece = rows[:, v * LANES : (v + 1) * LANES]
        ref[v, pl.ds(first, rows.shape[0], stride=step), :] = piece


def whole_rows(ref):
    return jnp.concatenate([ref[v] for v in range(ref.shape[0])], 1)


def factor_kernel(
    count, width, place_ref, s_ref, high_ref, low_ref, diag_ref, z_ref, lt_ref, mix_ref
):
    row_count, height = s_ref.shape[0], s_ref.shape[1]
    for p in range(row_count):
        interleave(mix_ref, p, row_count, s_ref[p])
    place = slot_place(count, width, place_ref[1])
    s = jnp.dot(whole_rows(mix_ref), place, precision=HI, preferred_element_type=F32)
    r = iota((KW, KW), 0)
    c = iota((KW, KW), 1)
    z_ref[:, :KW] = jnp.where(r >= c, s, 0.0) + jnp.where(r > c, s, 0.0).T
    z_ref[:, KW:] = (r == c).astype(F32)
    rows = iota((BLOCK, 1), 0)
    for b in range(KW // BLOCK):
        top = b * BLOCK
        strip = z_ref[top : top + BLOCK, :]
        scale = jnp.zeros((BLOCK, 1), F32)
        for j in range(BLOCK):
            col = strip[:, top + j : top + j + 1]
            row = strip[j : j + 1, :]
            pivot = strip[j : j + 1, top + j : top + j + 1]
            ratio = jnp.where(rows > j, col / pivot, 0.0)
            scale = jnp.where(rows == j, lax.rsqrt(pivot), scale)
            strip = strip - ratio * row
        strip = strip * scale
        z_ref[top : top + BLOCK, :] = strip
        lt_ref[top : top + BLOCK, :] = strip[:, :KW]
        if top + BLOCK < KW:
            update = lax.dot_general(
                strip[:, :KW], strip, (((0,), (0,)), ((), ())), precision=HI,
                preferred_element_type=F32,
            )
            z_ref[top + BLOCK :, :] = z_ref[top + BLOCK :, :] - update[top + BLOCK :, :]
    contract_last = (((1,), (1,)), ((), ()))
    inverse = z_ref[:, KW:]
    inverse = jnp.where(r >= c, inverse, 0.0)
    weights = lax.dot_general(
        place, inverse, contract_last, precision=HI, preferred_element_type=F32
    )
    high_ref[...], low_ref[...] = split(weights)
    upper = jnp.where(r <= c, lt_ref[...], 0.0)
    pick = iota((height, KW), 1) == iota((height, KW), 0) * row_count + place_ref[0]
    diag_ref[...] = lax.dot_general(
        pick.astype(F32), upper, contract_last, precision=HI, preferred_element_type=F32
    )


def factor_call(place, gathered, count, width):
    row_count, height = gathered.shape[0], gathered.shape[1]
    whole = lambda *shape: pl.BlockSpec(shape, lambda i, place: (0,) * len(shape))
    return pl.pallas_call(
        functools.partial(factor_kernel, count, width),
        grid_spec=pltpu.PrefetchScalarGridSpec(
            num_scalar_prefetch=1,
            grid=(1,),
            in_specs=[whole(row_count, height, KW)],
            out_specs=[whole(KW, KW), whole(KW, KW), whole(height, KW)],
            scratch_shapes=[
                pltpu.VMEM((KW, 2 * KW), F32),
                pltpu.VMEM((KW, KW), F32),
                pltpu.VMEM((KW // LANES, KW, LANES), F32),
            ],
        ),
        out_shape=[
            jax.ShapeDtypeStruct((KW, KW), BF16),
            jax.ShapeDtypeStruct((KW, KW), BF16),
            jax.ShapeDtypeStruct((height, KW), F32),
        ],
        compiler_params=PARAMS,
        name="factor",
    )(place, gathered)


def columns_kernel(count, width, place_ref, head_ref, nh_ref, nl_ref, high_ref, low_ref, scr_ref):
    groups = head_ref.shape[0]
    tiles = head_ref.shape[1]
    height = head_ref.shape[3] * (LANES // width)
    for a in range(groups):
        for t in range(tiles):
            raw = unpack([head_ref[a, t, s] for s in range(count)], width)
            panel = dot3(raw, nh_ref[...], nl_ref[...])
            interleave(scr_ref, t * height * groups + a, groups, panel)
    cols = scr_ref.shape[1]
    l = iota((cols, KW), 0)
    c = iota((cols, KW), 1)
    pick = jnp.where(c == l * count + place_ref[1], -1.0, 0.0)
    weights = jnp.where(l < width, pick, whole_rows(scr_ref)).T
    high_ref[...], low_ref[...] = split(weights)


def columns_call(place, head, n_high, n_low, count, width, cols):
    whole = lambda *shape: pl.BlockSpec(shape, lambda i, place: (0,) * len(shape))
    return pl.pallas_call(
        functools.partial(columns_kernel, count, width),
        grid_spec=pltpu.PrefetchScalarGridSpec(
            num_scalar_prefetch=1,
            grid=(1,),
            in_specs=[whole(*head.shape), whole(KW, KW), whole(KW, KW)],
            out_specs=[whole(KW, cols), whole(KW, cols)],
            scratch_shapes=[pltpu.VMEM((KW // LANES, cols, LANES), F32)],
        ),
        out_shape=[jax.ShapeDtypeStruct((KW, cols), BF16)] * 2,
        compiler_params=PARAMS,
        name="columns",
    )(place, head, n_high, n_low)


def update_kernel(count, width, row_count, head, aliased, place_ref, *refs):
    slots_in = refs[: 2 * count - 1]
    nh_ref, nl_ref, wh_ref, wl_ref, diag_ref, win_ref = refs[2 * count - 1 : 2 * count + 5]
    out_ref = refs[-1]
    p, q = place_ref[0], place_ref[1]
    slots = [slots_in[0][...]]
    for s in range(1, count):
        slots.append(jnp.where(q >= s, slots_in[s][...], slots_in[2 * count - 1 - s][...]))
    panel = dot3(unpack(slots, width), nh_ref[...], nl_ref[...])
    tile = panel.shape[0]
    lane = iota((tile, LANES), 1)
    row = iota((tile, LANES), 0)
    if head:
        height = diag_ref.shape[0]
        first = pl.program_id(0) == 0
        top = jnp.where(first, diag_ref[...], panel[:height])
        panel = jnp.concatenate([top, panel[height:]], 0)
        global_row = (row + pl.program_id(0) * tile) * row_count + p
    high, low = split(panel)
    dot = functools.partial(jnp.dot, preferred_element_type=F32)
    groups = wh_ref.shape[1] // LANES
    for pair in range(groups // 2):
        span = slice(pair * 2 * LANES, (pair + 1) * 2 * LANES)
        w_high, w_low = wh_ref[:, span], wl_ref[:, span]
        update = dot(high, w_high) + (dot(high, w_low) + dot(low, w_high))
        for half in range(2):
            g = pair * 2 + half
            old = win_ref[pl.ds(g, tile, stride=groups), :]
            if g * LANES < width:
                old = jnp.where(lane < width - g * LANES, 0.0, old)
            new = old - update[:, half * LANES : (half + 1) * LANES]
            if head:
                global_col = (lane + g * LANES) * count + q
                new = jnp.where(global_row >= global_col, new, 0.0)
            out_ref[pl.ds(g, tile, stride=groups), :] = new


def update_call(place, chunk, weights, flat, out, first, rows, tile, count, width, row_count):
    fold = LANES // width
    groups = weights[2].shape[1] // LANES
    base = first // tile
    whole = lambda x: pl.BlockSpec(x.shape, lambda i, place: (0,) * x.ndim)
    part = (tile // fold, LANES)
    specs = [pl.BlockSpec(part, lambda i, place: (i, 0))]
    for s in range(1, count):
        index = lambda i, place, s=s: (jnp.where(place[1] >= s, i, 0), 0)
        specs.append(pl.BlockSpec(part, index))
    for s in range(1, count):
        index = lambda i, place, s=s: (jnp.where(place[1] < count - s, i, 0), 0)
        specs.append(pl.BlockSpec(part, index))
    wide = pl.BlockSpec((tile * groups, LANES), lambda i, place: (base + i, 0))
    specs += [whole(x) for x in weights] + [wide]
    operands = [*chunk, *weights, flat]
    aliases = {}
    if out is not None:
        specs.append(pl.BlockSpec(memory_space=pl.ANY))
        operands.append(out)
        aliases = {len(operands): 0}
    kernel = functools.partial(
        update_kernel, count, width, row_count, first == 0, out is not None
    )
    return pl.pallas_call(
        kernel,
        grid_spec=pltpu.PrefetchScalarGridSpec(
            num_scalar_prefetch=1,
            grid=(rows // tile,),
            in_specs=specs,
            out_specs=wide,
        ),
        out_shape=jax.ShapeDtypeStruct(flat.shape, F32),
        input_output_aliases=aliases,
        compiler_params=PARAMS,
        cost_estimate=pl.CostEstimate(
            flops=6 * rows * KW * (KW + groups * LANES),
            bytes_accessed=rows * 4 * (2 * groups * LANES + KW),
            transcendentals=0,
        ),
        name="update",
    )(place, *operands)


def chunk_sizes(rest, tile):
    units = rest // tile
    sizes = []
    for share in (3, 3, 3):
        take = min(units, max(1, -(-rest // tile * share // 10)))
        if take:
            sizes.append(take * tile)
        units -= take
    if units:
        sizes.append(units * tile)
    return sizes


def body(window):
    local_rows = window.shape[1]
    local_cols = window.shape[3]
    row_count = lax.axis_size("row")
    count = lax.axis_size("col")
    p = lax.axis_index("row")
    q = lax.axis_index("col")
    width = KW // count
    height = KW // row_count
    head_rows = local_cols * count // row_count
    groups = row_count // count
    tile = min(TILE, head_rows)
    place = jnp.stack([p, q]).astype(jnp.int32)
    flat = window.reshape(local_rows * local_cols // LANES, LANES)

    sizes = [head_rows] + chunk_sizes(local_rows - head_rows, tile)
    starts = [sum(sizes[:i]) for i in range(len(sizes))]
    packed = [pack_rows(window, f, r, tile, width) for f, r in zip(starts, sizes)]

    ups = [[x] for x in packed]
    downs = [[x] for x in packed]

    def hop(j, s):
        up = [(i, i + 1) for i in range(s, count - 1)]
        down = [(i + 1, i) for i in range(count - 1 - s)]
        ups[j].append(lax.ppermute(ups[j][-1], "col", up))
        downs[j].append(lax.ppermute(downs[j][-1], "col", down))

    for s in range(count - 1):
        hop(0, s)
    for s in range(count - 1):
        for j in range(1, len(sizes)):
            hop(j, s)

    mine = [packed[0]]
    for s in range(1, count):
        mine.append(jnp.where(q >= s, ups[0][s], downs[0][count - s]))
    mine = jnp.stack(mine)

    lead = mine[:, : tile // (LANES // width)][:, :height, :width]
    lead = lead.transpose(1, 0, 2).reshape(height, KW)
    gathered = lax.all_gather(lead, "row")
    n_high, n_low, diag = factor_call(place, gathered, count, width)

    spread = mine
    bit = 1
    while bit < count:
        pairs = [(i, i ^ bit) for i in range(row_count)]
        other = lax.ppermute(spread, "row", pairs)
        spread = jnp.where(((p ^ q) & bit) != 0, other, spread)
        bit *= 2
    spread = spread[None]
    while bit < row_count:
        pairs = [(i, i ^ bit) for i in range(row_count)]
        other = lax.ppermute(spread, "row", pairs)
        low = (p & bit) == 0
        spread = jnp.concatenate(
            [jnp.where(low, spread, other), jnp.where(low, other, spread)], 0
        )
        bit *= 2
    fold = LANES // width
    spread = spread.reshape(groups, count, head_rows // tile, tile // fold, LANES)
    spread = spread.transpose(0, 2, 1, 3, 4)
    w_high, w_low = columns_call(place, spread, n_high, n_low, count, width, local_cols)

    weights = [n_high, n_low, w_high, w_low, diag]
    out = None
    for j, (first, rows) in enumerate(zip(starts, sizes)):
        chunk = [packed[j]] + ups[j][1:] + downs[j][1:]
        out = update_call(
            place, chunk, weights, flat, out, first, rows, tile, count, width, row_count
        )
    return out.reshape(window.shape)


def solution(mesh):
    spec = P("row", None, "col", None)
    return jax.shard_map(body, mesh=mesh, in_specs=(spec,), out_specs=spec, check_vma=False)
```

profile of v0, /device:TPU:16, one launch (start us, length us, event | category | flops | bytes accessed | tf_op | source)
XLA Modules:
  0.0 205.6 jit_solution(13399297686614262971)
XLA Ops:
  1.1 3.5 %collective-permute-start.6 = (f32[256,128]{1,0:T(8,128)S(1)}, f32[256,128]{1,0:T(8,128)S(1)}, u32[]{:S(2)}, u32[]{:S(2)}) collective-permute-start(f32[256,128]{1,0:T(8,128)S(1)} %pack.5.refs_0_), channel_id=1, source_target_pairs={{0,1},{1,2},{2,3},{4,5},{5,6},{6,7},{8,9},{9,10},{10,11},{12,13},{... | collective-permute-start | bytes 393224 | tf_op jit(solution)/shard_map/ppermute | solution.py:324
  4.6 2.4 %collective-permute-start.7 = (f32[256,128]{1,0:T(8,128)S(1)}, f32[256,128]{1,0:T(8,128)S(1)}, u32[]{:S(2)}, u32[]{:S(2)}) collective-permute-start(f32[256,128]{1,0:T(8,128)S(1)} %pack.5.refs_0_), channel_id=1, source_target_pairs={{1,0},{2,1},{3,2},{5,4},{6,5},{7,6},{9,8},{10,9},{11,10},{13,12},{... | collective-permute-start | bytes 393224 | tf_op jit(solution)/shard_map/ppermute | solution.py:325
  8.2 3.5 %collective-permute-start.10 = (f32[256,128]{1,0:T(8,128)S(1)}, f32[256,128]{1,0:T(8,128)S(1)}, u32[]{:S(2)}, u32[]{:S(2)}) collective-permute-start(f32[256,128]{1,0:T(8,128)S(1)} %collective-permute-done.6.refs_1_), channel_id=1, source_target_pairs={{1,2},{2,3},{5,6},{6,7},{9,10},{10,11},{13,14},{14,15},{17,18},{18... | collective-permute-start | bytes 393224 | tf_op jit(solution)/shard_map/ppermute | solution.py:324
  11.7 2.4 %collective-permute-start.8 = (f32[256,128]{1,0:T(8,128)S(1)}, f32[256,128]{1,0:T(8,128)S(1)}, u32[]{:S(2)}, u32[]{:S(2)}) collective-permute-start(f32[256,128]{1,0:T(8,128)S(1)} %collective-permute-done.7.refs_4_), channel_id=1, source_target_pairs={{1,0},{2,1},{5,4},{6,5},{9,8},{10,9},{13,12},{14,13},{17,16},{18,1... | collective-permute-start | bytes 393224 | tf_op jit(solution)/shard_map/ppermute | solution.py:325
  15.1 3.5 %collective-permute-start.11 = (f32[256,128]{1,0:T(8,128)S(1)}, f32[256,128]{1,0:T(8,128)S(1)}, u32[]{:S(2)}, u32[]{:S(2)}) collective-permute-start(f32[256,128]{1,0:T(8,128)S(1)} %collective-permute-done.10.refs_2_), channel_id=1, source_target_pairs={{2,3},{6,7},{10,11},{14,15},{18,19},{22,23},{26,27},{30,31}} | collective-permute-start | bytes 393224 | tf_op jit(solution)/shard_map/ppermute | solution.py:324
  22.0 3.3 %pack.7.refs_0_ = f32[1280,128]{1,0:T(8,128)S(1)} custom-call(f32[1,8192,1,1024]{3,2,1,0:T(1,128)} %win_ref.7), custom_call_target="tpu_custom_call" | custom-call | tf_op jit(solution)/shard_map/pack/pallas_call | solution.py:51
  25.3 4.4 %collective-permute-start.21 = (f32[1280,128]{1,0:T(8,128)S(1)}, f32[1280,128]{1,0:T(8,128)}, u32[]{:S(2)}, u32[]{:S(2)}) collective-permute-start(f32[1280,128]{1,0:T(8,128)S(1)} %pack.7.refs_0_), channel_id=1, source_target_pairs={{0,1},{1,2},{2,3},{4,5},{5,6},{6,7},{8,9},{9,10},{10,11},{12,13},{... | collective-permute-start | bytes 1966088 | tf_op jit(solution)/shard_map/ppermute | solution.py:324
  29.7 1.9 collective-permute-start.24
  31.7 3.3 %pack.6.refs_0_ = f32[1280,128]{1,0:T(8,128)S(1)} custom-call(f32[1,8192,1,1024]{3,2,1,0:T(1,128)} %win_ref.7), custom_call_target="tpu_custom_call" | custom-call | tf_op jit(solution)/shard_map/pack/pallas_call | solution.py:51
  35.0 4.7 %collective-permute-start.15 = (f32[1280,128]{1,0:T(8,128)S(1)}, f32[1280,128]{1,0:T(8,128)S(1)}, u32[]{:S(2)}, u32[]{:S(2)}) collective-permute-start(f32[1280,128]{1,0:T(8,128)S(1)} %pack.6.refs_0_), channel_id=1, source_target_pairs={{0,1},{1,2},{2,3},{4,5},{5,6},{6,7},{8,9},{9,10},{10,11},{12,13},{... | collective-permute-start | bytes 1966088 | tf_op jit(solution)/shard_map/ppermute | solution.py:324
  39.8 1.9 collective-permute-start.18
  41.7 2.0 broadcast_select_fusion
  45.3 3.3 %pack.4.refs_0_ = f32[1280,128]{1,0:T(8,128)S(1)} custom-call(f32[1,8192,1,1024]{3,2,1,0:T(1,128)} %win_ref.7), custom_call_target="tpu_custom_call" | custom-call | tf_op jit(solution)/shard_map/pack/pallas_call | solution.py:51
  48.5 4.0 %collective-permute-start = (f32[1280,128]{1,0:T(8,128)S(1)}, f32[1280,128]{1,0:T(8,128)}, u32[]{:S(2)}, u32[]{:S(2)}) collective-permute-start(f32[1280,128]{1,0:T(8,128)S(1)} %pack.4.refs_0_), channel_id=1, source_target_pairs={{0,1},{1,2},{2,3},{4,5},{5,6},{6,7},{8,9},{9,10},{10,11},{12,13},{... | collective-permute-start | bytes 1966088 | tf_op jit(solution)/shard_map/ppermute | solution.py:324
  52.5 1.9 collective-permute-start.3
  54.5 4.8 %collective-permute-done.15.refs_1_ = f32[1280,128]{1,0:T(8,128)S(1)} collective-permute-done((f32[1280,128]{1,0:T(8,128)S(1)}, f32[1280,128]{1,0:T(8,128)S(1)}, u32[]{:S(2)}, u32[]{:S(2)}) %collective-permute-start.15) | collective-permute-done | bytes 655392 | tf_op jit(solution)/shard_map/ppermute | solution.py:324
  59.3 3.8 %collective-permute-start.22 = (f32[1280,128]{1,0:T(8,128)}, f32[1280,128]{1,0:T(8,128)}, u32[]{:S(2)}, u32[]{:S(2)}) collective-permute-start(f32[1280,128]{1,0:T(8,128)} %collective-permute-done.21.refs_1_), channel_id=1, source_target_pairs={{1,2},{2,3},{5,6},{6,7},{9,10},{10,11},{13,14},{14,15},{17,18},{18... | collective-permute-start | bytes 1966088 | tf_op jit(solution)/shard_map/ppermute | solution.py:324
  63.2 3.6 %collective-permute-start.25 = (f32[1280,128]{1,0:T(8,128)}, f32[1280,128]{1,0:T(8,128)}, u32[]{:S(2)}, u32[]{:S(2)}) collective-permute-start(f32[1280,128]{1,0:T(8,128)} %collective-permute-done.24.refs_4_), channel_id=1, source_target_pairs={{1,0},{2,1},{5,4},{6,5},{9,8},{10,9},{13,12},{14,13},{17,16},{18,1... | collective-permute-start | bytes 1966088 | tf_op jit(solution)/shard_map/ppermute | solution.py:325
  68.8 2.0 select_bitcast_fusion
  70.8 2.7 %collective-permute-done.refs_1_ = f32[1280,128]{1,0:T(8,128)} collective-permute-done((f32[1280,128]{1,0:T(8,128)S(1)}, f32[1280,128]{1,0:T(8,128)}, u32[]{:S(2)}, u32[]{:S(2)}) %collective-permute-start) | collective-permute-done | bytes 655392 | tf_op jit(solution)/shard_map/ppermute | solution.py:324
  76.7 3.7 %collective-permute-start.19 = (f32[1280,128]{1,0:T(8,128)S(1)}, f32[1280,128]{1,0:T(8,128)}, u32[]{:S(2)}, u32[]{:S(2)}) collective-permute-start(f32[1280,128]{1,0:T(8,128)S(1)} %collective-permute-done.18.refs_4_), channel_id=1, source_target_pairs={{1,0},{2,1},{5,4},{6,5},{9,8},{10,9},{13,12},{14,13},{17,16},{18,1... | collective-permute-start | bytes 1966088 | tf_op jit(solution)/shard_map/ppermute | solution.py:325
  80.4 7.1 %collective-permute-done.22.refs_2_ = f32[1280,128]{1,0:T(8,128)} collective-permute-done((f32[1280,128]{1,0:T(8,128)}, f32[1280,128]{1,0:T(8,128)}, u32[]{:S(2)}, u32[]{:S(2)}) %collective-permute-start.22) | collective-permute-done | bytes 655392 | tf_op jit(solution)/shard_map/ppermute | solution.py:324
  87.5 3.8 %collective-permute-start.1 = (f32[1280,128]{1,0:T(8,128)}, f32[1280,128]{1,0:T(8,128)}, u32[]{:S(2)}, u32[]{:S(2)}) collective-permute-start(f32[1280,128]{1,0:T(8,128)} %collective-permute-done.refs_1_), channel_id=1, source_target_pairs={{1,2},{2,3},{5,6},{6,7},{9,10},{10,11},{13,14},{14,15},{17,18},{18... | collective-permute-start | bytes 1966088 | tf_op jit(solution)/shard_map/ppermute | solution.py:324
  91.4 3.7 %collective-permute-start.4 = (f32[1280,128]{1,0:T(8,128)}, f32[1280,128]{1,0:T(8,128)}, u32[]{:S(2)}, u32[]{:S(2)}) collective-permute-start(f32[1280,128]{1,0:T(8,128)} %collective-permute-done.3.refs_4_), channel_id=1, source_target_pairs={{1,0},{2,1},{5,4},{6,5},{9,8},{10,9},{13,12},{14,13},{17,16},{18,1... | collective-permute-start | bytes 1966088 | tf_op jit(solution)/shard_map/ppermute | solution.py:325
  95.1 6.4 %collective-permute-done.16.refs_2_ = f32[1280,128]{1,0:T(8,128)} collective-permute-done((f32[1280,128]{1,0:T(8,128)S(1)}, f32[1280,128]{1,0:T(8,128)}, u32[]{:S(2)}, u32[]{:S(2)}) %collective-permute-start.16) | collective-permute-done | bytes 655392 | tf_op jit(solution)/shard_map/ppermute | solution.py:324
  101.5 4.6 %collective-permute-start.23 = (f32[1280,128]{1,0:T(8,128)}, f32[1280,128]{1,0:T(8,128)}, u32[]{:S(2)}, u32[]{:S(2)}) collective-permute-start(f32[1280,128]{1,0:T(8,128)} %collective-permute-done.22.refs_2_), channel_id=1, source_target_pairs={{2,3},{6,7},{10,11},{14,15},{18,19},{22,23},{26,27},{30,31}} | collective-permute-start | bytes 1966088 | tf_op jit(solution)/shard_map/ppermute | solution.py:324
  110.8 9.7 %all_gather.3.s_ref = f32[8,32,256]{2,1,0:T(8,128)S(1)} all-gather(f32[1,32,256]{2,1,0:T(8,128)} %all_gather_reshape.3), channel_id=1, replica_groups=mesh['row'=8,'col'=4] {'row'}, dimensions={0}, use_global_device_ids=true | all-gather | bytes 294912 | tf_op jit(solution)/shard_map/all_gather | solution.py:340
  120.5 27.8 %factor.1 = (bf16[256,256]{1,0:T(8,128)(2,1)S(1)}, bf16[256,256]{1,0:T(8,128)(2,1)S(1)}, f32[32,256]{1,0:T(8,128)S(1)}) custom-call(s32[2]{0:T(128)S(1)} %pad_add_fusion.place_ref, f32[8,32,256]{2,1,0:T(8,128)S(1)} %all_gather.3.s_ref), custom_call_target="tpu_custom_call" | custom-call | tf_op jit(solution)/shard_map/factor/pallas_call | solution.py:148
  158.0 5.1 %update.4.refs_13_ = f32[65536,128]{1,0:T(8,128)} custom-call(s32[2]{0:T(128)S(1)} %pad_add_fusion.place_ref, f32[256,128]{1,0:T(8,128)S(1)} %pack.5.refs_0_, f32[256,128]{1,0:T(8,128)S(1)} %collective-permute-done.6.refs_1_, f32[256,128]{1,0:T(8,128)S(1)} %copy-done.3, f32[256,128]{1,0:T(8,128)S(1)} %copy-done.7, f32[256,128]{1,0:T(8,128)S(1)} %copy-done.1, ...), custom_call_target="tpu_custom_call" | custom-call | flops 1006632960 | bytes 4718592 | tf_op jit(solution)/shard_map/update/pallas_call | solution.py:266
  165.1 13.7 %update.5.refs_13_ = f32[65536,128]{1,0:T(8,128)} custom-call(s32[2]{0:T(128)S(1)} %pad_add_fusion.place_ref, f32[1280,128]{1,0:T(8,128)S(1)} %pack.7.refs_0_, f32[1280,128]{1,0:T(8,128)} %collective-permute-done.21.refs_1_, f32[1280,128]{1,0:T(8,128)} %collective-permute-done.22.refs_2_, ...), custom_call_target="tpu_custom_call", output_to_operand_aliasing={{}: (14, {})} | custom-call | flops 5033164800 | bytes 23592960 | tf_op jit(solution)/shard_map/update/pallas_call | solution.py:266
  178.8 13.2 %update.6.refs_13_ = f32[65536,128]{1,0:T(8,128)} custom-call(s32[2]{0:T(128)S(1)} %pad_add_fusion.place_ref, f32[1280,128]{1,0:T(8,128)S(1)} %pack.6.refs_0_, f32[1280,128]{1,0:T(8,128)S(1)} %collective-permute-done.15.refs_1_, f32[1280,128]{1,0:T(8,128)} %collective-permute-done.16.refs_2_, ...), custom_call_target="tpu_custom_call", output_to_operand_aliasing={{}: (14, {})} | custom-call | flops 5033164800 | bytes 23592960 | tf_op jit(solution)/shard_map/update/pallas_call | solution.py:266
  192.0 13.5 %update.7 = f32[65536,128]{1,0:T(8,128)} custom-call(s32[2]{0:T(128)S(1)} %pad_add_fusion.place_ref, f32[1280,128]{1,0:T(8,128)S(1)} %pack.4.refs_0_, f32[1280,128]{1,0:T(8,128)} %collective-permute-done.refs_1_, f32[1280,128]{1,0:T(8,128)} %collective-permute-done.1.refs_2_, ...), custom_call_target="tpu_custom_call", output_to_operand_aliasing={{}: (14, {})} | custom-call | flops 5033164800 | bytes 23592960 | tf_op jit(solution)/shard_map/update/pallas_call | solution.py:266
  (75 shorter events, 29.9 us)
Async XLA Ops:
  1.1 7.1 %collective-permute-start.6 = (f32[256,128]{1,0:T(8,128)S(1)}, f32[256,128]{1,0:T(8,128)S(1)}, u32[]{:S(2)}, u32[]{:S(2)}) collective-permute-start(f32[256,128]{1,0:T(8,128)S(1)} %pack.5.refs_0_), channel_id=1, source_target_pairs={{0,1},{1,2},{2,3},{4,5},{5,6},{6,7},{8,9},{9,10},{10,11},{12,13},{... | collective-permute-start | bytes 393224 | tf_op jit(solution)/shard_map/ppermute | solution.py:324
  4.6 7.1 %collective-permute-start.7 = (f32[256,128]{1,0:T(8,128)S(1)}, f32[256,128]{1,0:T(8,128)S(1)}, u32[]{:S(2)}, u32[]{:S(2)}) collective-permute-start(f32[256,128]{1,0:T(8,128)S(1)} %pack.5.refs_0_), channel_id=1, source_target_pairs={{1,0},{2,1},{3,2},{5,4},{6,5},{7,6},{9,8},{10,9},{11,10},{13,12},{... | collective-permute-start | bytes 393224 | tf_op jit(solution)/shard_map/ppermute | solution.py:325
  8.2 6.8 %collective-permute-start.10 = (f32[256,128]{1,0:T(8,128)S(1)}, f32[256,128]{1,0:T(8,128)S(1)}, u32[]{:S(2)}, u32[]{:S(2)}) collective-permute-start(f32[256,128]{1,0:T(8,128)S(1)} %collective-permute-done.6.refs_1_), channel_id=1, source_target_pairs={{1,2},{2,3},{5,6},{6,7},{9,10},{10,11},{13,14},{14,15},{17,18},{18... | collective-permute-start | bytes 393224 | tf_op jit(solution)/shard_map/ppermute | solution.py:324
  11.7 18.0 %copy-start = (f32[256,128]{1,0:T(8,128)}, f32[256,128]{1,0:T(8,128)S(1)}, u32[]{:S(2)}) copy-start(f32[256,128]{1,0:T(8,128)S(1)} %collective-permute-done.7.refs_4_) | copy-start | bytes 393220
  11.7 6.8 %collective-permute-start.8 = (f32[256,128]{1,0:T(8,128)S(1)}, f32[256,128]{1,0:T(8,128)S(1)}, u32[]{:S(2)}, u32[]{:S(2)}) collective-permute-start(f32[256,128]{1,0:T(8,128)S(1)} %collective-permute-done.7.refs_4_), channel_id=1, source_target_pairs={{1,0},{2,1},{5,4},{6,5},{9,8},{10,9},{13,12},{14,13},{17,16},{18,1... | collective-permute-start | bytes 393224 | tf_op jit(solution)/shard_map/ppermute | solution.py:325
  15.1 14.6 %copy-start.2 = (f32[256,128]{1,0:T(8,128)}, f32[256,128]{1,0:T(8,128)S(1)}, u32[]{:S(2)}) copy-start(f32[256,128]{1,0:T(8,128)S(1)} %collective-permute-done.10.refs_2_) | copy-start | bytes 393220
  15.1 6.0 %collective-permute-start.11 = (f32[256,128]{1,0:T(8,128)S(1)}, f32[256,128]{1,0:T(8,128)S(1)}, u32[]{:S(2)}, u32[]{:S(2)}) collective-permute-start(f32[256,128]{1,0:T(8,128)S(1)} %collective-permute-done.10.refs_2_), channel_id=1, source_target_pairs={{2,3},{6,7},{10,11},{14,15},{18,19},{22,23},{26,27},{30,31}} | collective-permute-start | bytes 393224 | tf_op jit(solution)/shard_map/ppermute | solution.py:324
  18.6 11.1 %copy-start.4 = (f32[256,128]{1,0:T(8,128)}, f32[256,128]{1,0:T(8,128)S(1)}, u32[]{:S(2)}) copy-start(f32[256,128]{1,0:T(8,128)S(1)} %collective-permute-done.8.refs_5_) | copy-start | bytes 393220
  18.6 2.5 %collective-permute-start.9 = (f32[256,128]{1,0:T(8,128)S(1)}, f32[256,128]{1,0:T(8,128)S(1)}, u32[]{:S(2)}, u32[]{:S(2)}) collective-permute-start(f32[256,128]{1,0:T(8,128)S(1)} %collective-permute-done.8.refs_5_), channel_id=1, source_target_pairs={{1,0},{5,4},{9,8},{13,12},{17,16},{21,20},{25,24},{29,28}} | collective-permute-start | bytes 393224 | tf_op jit(solution)/shard_map/ppermute | solution.py:325
  19.3 10.4 %copy-start.11 = (f32[1,256,128]{2,1,0:T(8,128)}, f32[1,256,128]{2,1,0:T(8,128)S(1)}, u32[]{:S(2)}) copy-start(f32[1,256,128]{2,1,0:T(8,128)S(1)} %select_bitcast_fusion.2) | copy-start | bytes 393220
  22.0 19.7 %collective-permute-start.12 = (f32[4,256,128]{2,1,0:T(8,128)}, f32[4,256,128]{2,1,0:T(8,128)S(1)}, u32[]{:S(2)}, u32[]{:S(2)}) collective-permute-start(f32[4,256,128]{2,1,0:T(8,128)} %pad_maximum_fusion), channel_id=1, source_target_pairs={{0,4},{4,0},{8,12},{12,8},{16,20},{20,16},{24,28},{28,24},{1,5},{5... | collective-permute-start | bytes 1572872 | tf_op jit(solution)/shard_map/ppermute | solution.py:347
  25.3 23.2 %collective-permute-start.21 = (f32[1280,128]{1,0:T(8,128)S(1)}, f32[1280,128]{1,0:T(8,128)}, u32[]{:S(2)}, u32[]{:S(2)}) collective-permute-start(f32[1280,128]{1,0:T(8,128)S(1)} %pack.7.refs_0_), channel_id=1, source_target_pairs={{0,1},{1,2},{2,3},{4,5},{5,6},{6,7},{8,9},{9,10},{10,11},{12,13},{... | collective-permute-start | bytes 1966088 | tf_op jit(solution)/shard_map/ppermute | solution.py:324
  29.7 22.8 %collective-permute-start.24 = (f32[1280,128]{1,0:T(8,128)S(1)}, f32[1280,128]{1,0:T(8,128)}, u32[]{:S(2)}, u32[]{:S(2)}) collective-permute-start(f32[1280,128]{1,0:T(8,128)S(1)} %pack.7.refs_0_), channel_id=1, source_target_pairs={{1,0},{2,1},{3,2},{5,4},{6,5},{7,6},{9,8},{10,9},{11,10},{13,12},{... | collective-permute-start | bytes 1966088 | tf_op jit(solution)/shard_map/ppermute | solution.py:325
  31.7 10.0 %copy-start.12 = (f32[1,256,128]{2,1,0:T(8,128)S(1)}, f32[1,256,128]{2,1,0:T(8,128)}, u32[]{:S(2)}) copy-start(f32[1,256,128]{2,1,0:T(8,128)} %copy-done.11) | copy-start | bytes 393220
  35.0 24.3 %collective-permute-start.15 = (f32[1280,128]{1,0:T(8,128)S(1)}, f32[1280,128]{1,0:T(8,128)S(1)}, u32[]{:S(2)}, u32[]{:S(2)}) collective-permute-start(f32[1280,128]{1,0:T(8,128)S(1)} %pack.6.refs_0_), channel_id=1, source_target_pairs={{0,1},{1,2},{2,3},{4,5},{5,6},{6,7},{8,9},{9,10},{10,11},{12,13},{... | collective-permute-start | bytes 1966088 | tf_op jit(solution)/shard_map/ppermute | solution.py:324
  39.8 23.5 %collective-permute-start.18 = (f32[1280,128]{1,0:T(8,128)S(1)}, f32[1280,128]{1,0:T(8,128)S(1)}, u32[]{:S(2)}, u32[]{:S(2)}) collective-permute-start(f32[1280,128]{1,0:T(8,128)S(1)} %pack.6.refs_0_), channel_id=1, source_target_pairs={{1,0},{2,1},{3,2},{5,4},{6,5},{7,6},{9,8},{10,9},{11,10},{13,12},{... | collective-permute-start | bytes 1966088 | tf_op jit(solution)/shard_map/ppermute | solution.py:325
  43.8 23.1 %collective-permute-start.13 = (f32[4,256,128]{2,1,0:T(8,128)}, f32[4,256,128]{2,1,0:T(8,128)}, u32[]{:S(2)}, u32[]{:S(2)}) collective-permute-start(f32[4,256,128]{2,1,0:T(8,128)} %broadcast_select_fusion), channel_id=1, source_target_pairs={{0,8},{4,12},{8,0},{12,4},{16,24},{20,28},{24,16},{28,20},{1,9},{5... | collective-permute-start | bytes 1572872 | tf_op jit(solution)/shard_map/ppermute | solution.py:347
  48.5 24.9 %collective-permute-start = (f32[1280,128]{1,0:T(8,128)S(1)}, f32[1280,128]{1,0:T(8,128)}, u32[]{:S(2)}, u32[]{:S(2)}) collective-permute-start(f32[1280,128]{1,0:T(8,128)S(1)} %pack.4.refs_0_), channel_id=1, source_target_pairs={{0,1},{1,2},{2,3},{4,5},{5,6},{6,7},{8,9},{9,10},{10,11},{12,13},{... | collective-permute-start | bytes 1966088 | tf_op jit(solution)/shard_map/ppermute | solution.py:324
  52.5 24.1 %collective-permute-start.3 = (f32[1280,128]{1,0:T(8,128)S(1)}, f32[1280,128]{1,0:T(8,128)}, u32[]{:S(2)}, u32[]{:S(2)}) collective-permute-start(f32[1280,128]{1,0:T(8,128)S(1)} %pack.4.refs_0_), channel_id=1, source_target_pairs={{1,0},{2,1},{3,2},{5,4},{6,5},{7,6},{9,8},{10,9},{11,10},{13,12},{... | collective-permute-start | bytes 1966088 | tf_op jit(solution)/shard_map/ppermute | solution.py:325
  59.3 28.2 %collective-permute-start.22 = (f32[1280,128]{1,0:T(8,128)}, f32[1280,128]{1,0:T(8,128)}, u32[]{:S(2)}, u32[]{:S(2)}) collective-permute-start(f32[1280,128]{1,0:T(8,128)} %collective-permute-done.21.refs_1_), channel_id=1, source_target_pairs={{1,2},{2,3},{5,6},{6,7},{9,10},{10,11},{13,14},{14,15},{17,18},{18... | collective-permute-start | bytes 1966088 | tf_op jit(solution)/shard_map/ppermute | solution.py:324
  63.2 28.2 %collective-permute-start.25 = (f32[1280,128]{1,0:T(8,128)}, f32[1280,128]{1,0:T(8,128)}, u32[]{:S(2)}, u32[]{:S(2)}) collective-permute-start(f32[1280,128]{1,0:T(8,128)} %collective-permute-done.24.refs_4_), channel_id=1, source_target_pairs={{1,0},{2,1},{5,4},{6,5},{9,8},{10,9},{13,12},{14,13},{17,16},{18,1... | collective-permute-start | bytes 1966088 | tf_op jit(solution)/shard_map/ppermute | solution.py:325
  66.8 34.7 %collective-permute-start.16 = (f32[1280,128]{1,0:T(8,128)S(1)}, f32[1280,128]{1,0:T(8,128)}, u32[]{:S(2)}, u32[]{:S(2)}) collective-permute-start(f32[1280,128]{1,0:T(8,128)S(1)} %collective-permute-done.15.refs_1_), channel_id=1, source_target_pairs={{1,2},{2,3},{5,6},{6,7},{9,10},{10,11},{13,14},{14,15},{17,18},{18... | collective-permute-start | bytes 1966088 | tf_op jit(solution)/shard_map/ppermute | solution.py:324
  73.5 32.7 %collective-permute-start.14 = (f32[1,4,256,128]{3,2,1,0:T(8,128)}, f32[1,4,256,128]{3,2,1,0:T(8,128)}, u32[]{:S(2)}, u32[]{:S(2)}) collective-permute-start(f32[1,4,256,128]{3,2,1,0:T(8,128)} %select_bitcast_fusion), channel_id=1, source_target_pairs={{0,16},{4,20},{8,24},{12,28},{16,0},{20,4},{24,8},{28,12},{1,17},{... | collective-permute-start | bytes 1572872 | tf_op jit(solution)/shard_map/ppermute | solution.py:353
  76.7 72.9 %collective-permute-start.19 = (f32[1280,128]{1,0:T(8,128)S(1)}, f32[1280,128]{1,0:T(8,128)}, u32[]{:S(2)}, u32[]{:S(2)}) collective-permute-start(f32[1280,128]{1,0:T(8,128)S(1)} %collective-permute-done.18.refs_4_), channel_id=1, source_target_pairs={{1,0},{2,1},{5,4},{6,5},{9,8},{10,9},{13,12},{14,13},{17,16},{18,1... | collective-permute-start | bytes 1966088 | tf_op jit(solution)/shard_map/ppermute | solution.py:325
  87.5 63.4 %collective-permute-start.1 = (f32[1280,128]{1,0:T(8,128)}, f32[1280,128]{1,0:T(8,128)}, u32[]{:S(2)}, u32[]{:S(2)}) collective-permute-start(f32[1280,128]{1,0:T(8,128)} %collective-permute-done.refs_1_), channel_id=1, source_target_pairs={{1,2},{2,3},{5,6},{6,7},{9,10},{10,11},{13,14},{14,15},{17,18},{18... | collective-permute-start | bytes 1966088 | tf_op jit(solution)/shard_map/ppermute | solution.py:324
  91.4 71.6 %collective-permute-start.4 = (f32[1280,128]{1,0:T(8,128)}, f32[1280,128]{1,0:T(8,128)}, u32[]{:S(2)}, u32[]{:S(2)}) collective-permute-start(f32[1280,128]{1,0:T(8,128)} %collective-permute-done.3.refs_4_), channel_id=1, source_target_pairs={{1,0},{2,1},{5,4},{6,5},{9,8},{10,9},{13,12},{14,13},{17,16},{18,1... | collective-permute-start | bytes 1966088 | tf_op jit(solution)/shard_map/ppermute | solution.py:325
  101.5 62.8 %collective-permute-start.23 = (f32[1280,128]{1,0:T(8,128)}, f32[1280,128]{1,0:T(8,128)}, u32[]{:S(2)}, u32[]{:S(2)}) collective-permute-start(f32[1280,128]{1,0:T(8,128)} %collective-permute-done.22.refs_2_), channel_id=1, source_target_pairs={{2,3},{6,7},{10,11},{14,15},{18,19},{22,23},{26,27},{30,31}} | collective-permute-start | bytes 1966088 | tf_op jit(solution)/shard_map/ppermute | solution.py:324
  106.2 58.9 %collective-permute-start.26 = (f32[1280,128]{1,0:T(8,128)}, f32[1280,128]{1,0:T(8,128)}, u32[]{:S(2)}, u32[]{:S(2)}) collective-permute-start(f32[1280,128]{1,0:T(8,128)} %collective-permute-done.25.refs_5_), channel_id=1, source_target_pairs={{1,0},{5,4},{9,8},{13,12},{17,16},{21,20},{25,24},{29,28}} | collective-permute-start | bytes 1966088 | tf_op jit(solution)/shard_map/ppermute | solution.py:325
  149.6 29.2 %collective-permute-start.17 = (f32[1280,128]{1,0:T(8,128)}, f32[1280,128]{1,0:T(8,128)S(1)}, u32[]{:S(2)}, u32[]{:S(2)}) collective-permute-start(f32[1280,128]{1,0:T(8,128)} %collective-permute-done.16.refs_2_), channel_id=1, source_target_pairs={{2,3},{6,7},{10,11},{14,15},{18,19},{22,23},{26,27},{30,31}} | collective-permute-start | bytes 1966088 | tf_op jit(solution)/shard_map/ppermute | solution.py:324
  150.9 27.8 %collective-permute-start.20 = (f32[1280,128]{1,0:T(8,128)}, f32[1280,128]{1,0:T(8,128)S(1)}, u32[]{:S(2)}, u32[]{:S(2)}) collective-permute-start(f32[1280,128]{1,0:T(8,128)} %collective-permute-done.19.refs_5_), channel_id=1, source_target_pairs={{1,0},{5,4},{9,8},{13,12},{17,16},{21,20},{25,24},{29,28}} | collective-permute-start | bytes 1966088 | tf_op jit(solution)/shard_map/ppermute | solution.py:325
  163.0 29.0 %collective-permute-start.2 = (f32[1280,128]{1,0:T(8,128)}, f32[1280,128]{1,0:T(8,128)S(1)}, u32[]{:S(2)}, u32[]{:S(2)}) collective-permute-start(f32[1280,128]{1,0:T(8,128)} %collective-permute-done.1.refs_2_), channel_id=1, source_target_pairs={{2,3},{6,7},{10,11},{14,15},{18,19},{22,23},{26,27},{30,31}} | collective-permute-start | bytes 1966088 | tf_op jit(solution)/shard_map/ppermute | solution.py:324
  164.4 27.6 %collective-permute-start.5 = (f32[1280,128]{1,0:T(8,128)}, f32[1280,128]{1,0:T(8,128)S(1)}, u32[]{:S(2)}, u32[]{:S(2)}) collective-permute-start(f32[1280,128]{1,0:T(8,128)} %collective-permute-done.4.refs_5_), channel_id=1, source_target_pairs={{1,0},{5,4},{9,8},{13,12},{17,16},{21,20},{25,24},{29,28}} | collective-permute-start | bytes 1966088 | tf_op jit(solution)/shard_map/ppermute | solution.py:325
  (10 other events, 25.7 us)
where the time goes:
time: 208 us; the launch traced here: 206 us
  Pallas kernels  85.7 us (41%)
  starting transfers between devices  68.7 us (33%)
  waiting for transfers between devices  26.9 us (13%)
  blocking collectives  9.69 us (5%)
  local copies, waits for them, and re-layouts  7.63 us (4%)
  other arithmetic  6.44 us (3%)
    pallas_call x4, Pallas kernels, update_call(): pl.pallas_call(kernel, grid_spec=pltpu.PrefetchScalarGridSpec(num_scalar_...  45.5 us
    ppermute x12, starting transfers between devices, hop(): ups[j].append(lax.ppermute(ups[j][-1], 'col', up))  40.3 us
    pallas_call x1, Pallas kernels, factor_call(): pl.pallas_call(functools.partial(factor_kernel, count, width), grid_spec=...  27.8 us
    ppermute x12, starting transfers between devices, hop(): downs[j].append(lax.ppermute(downs[j][-1], 'col', down))  25.4 us
    ppermute x12, waiting for transfers between devices, hop(): ups[j].append(lax.ppermute(ups[j][-1], 'col', up))  25 us
    pallas_call x4, Pallas kernels, pack_rows(): pl.pallas_call(functools.partial(pack_kernel, width), grid=(rows // tile,...  11 us
    all_gather x1, blocking collectives, body(): gathered = lax.all_gather(lead, 'row')  9.69 us
    unnamed x30, local copies, waits for them, and re-layouts  4.55 us
  transfers between devices with their start and end apart: 27, of which 9 were waited for; matrix products, arithmetic and copies ran while one was open for 4% of the time, Pallas kernels for 35%

commit v1 on v0

v1 whole, which is shorter than its diff:
```python
import functools

import jax
import jax.numpy as jnp
from jax import lax
from jax.experimental import pallas as pl
from jax.experimental.pallas import tpu as pltpu
from jax.sharding import PartitionSpec as P

NB = 128
KW = 2 * NB
LANES = 128
BLOCK = 32
TILE = 512
SHARES = (9, 4)
DEPTH = 6
F32 = jnp.float32
BF16 = jnp.bfloat16
HI = lax.Precision.HIGHEST
PARAMS = pltpu.CompilerParams(vmem_limit_bytes=32 * 1024 * 1024)

LIGHT = pl.CostEstimate(flops=0, bytes_accessed=0, transcendentals=0)


def iota(shape, dim):
    return lax.broadcasted_iota(jnp.int32, shape, dim)


def split(x):
    high = x.astype(BF16)
    return high, (x - high.astype(F32)).astype(BF16)


def dot3(a, b_high, b_low):
    a_high, a_low = split(a)
    dot = functools.partial(jnp.dot, preferred_element_type=F32)
    return dot(a_high, b_high) + (dot(a_high, b_low) + dot(a_low, b_high))


def pack_kernel(width, win_ref, out_ref):
    fold = LANES // width
    part = win_ref.shape[0] // fold
    tile = win_ref[:, 0, :]
    lane = iota((part, LANES), 1) // width
    out = tile[:part]
    for j in range(1, fold):
        rolled = pltpu.roll(tile[j * part : (j + 1) * part], j * width, 1)
        out = jnp.where(lane == j, rolled, out)
    out_ref[...] = out


def pack_rows(window, first, rows, tile, width):
    fold = LANES // width
    base = first // tile
    return pl.pallas_call(
        functools.partial(pack_kernel, width),
        grid=(rows // tile,),
        in_specs=[pl.BlockSpec((None, tile, 1, LANES), lambda i: (0, base + i, 0, 0))],
        out_specs=pl.BlockSpec((tile // fold, LANES), lambda i: (i, 0)),
        out_shape=jax.ShapeDtypeStruct((rows // fold, LANES), F32),
        compiler_params=PARAMS,
        cost_estimate=LIGHT,
        name="pack",
    )(window)


def unpack(slots, width):
    fold = LANES // width
    part = slots[0].shape[0]
    lane = iota((part, LANES), 1) // width
    rows = []
    for j in range(fold):
        pieces = []
        for v in range(len(slots) // fold):
            piece = None
            for m in range(fold):
                slot = slots[v * fold + m]
                shift = (m - j) % fold
                moved = pltpu.roll(slot, shift * width, 1) if shift else slot
                piece = moved if piece is None else jnp.where(lane == m, moved, piece)
            pieces.append(piece)
        rows.append(jnp.concatenate(pieces, 1))
    return jnp.concatenate(rows, 0)


def slot_place(count, width, col_index):
    a = iota((KW, KW), 0)
    c = iota((KW, KW), 1)
    source = lax.rem(col_index - a // width + count, count)
    return (c == lax.rem(a, width) * count + source).astype(F32)


def interleave(ref, first, step, rows):
    for v in range(ref.shape[0]):
        piece = rows[:, v * LANES : (v + 1) * LANES]
        ref[v, pl.ds(first, rows.shape[0], stride=step), :] = piece


def whole_rows(ref):
    return jnp.concatenate([ref[v] for v in range(ref.shape[0])], 1)


def eliminate(z_ref, lt_ref):
    rows = iota((BLOCK, 1), 0)
    for b in range(KW // BLOCK):
        top = b * BLOCK
        strip = z_ref[top : top + BLOCK, :]
        scale = jnp.zeros((BLOCK, 1), F32)
        for j in range(BLOCK):
            col = strip[:, top + j : top + j + 1]
            row = strip[j : j + 1, :]
            pivot = strip[j : j + 1, top + j : top + j + 1]
            ratio = jnp.where(rows > j, col / pivot, 0.0)
            scale = jnp.where(rows == j, lax.rsqrt(pivot), scale)
            strip = strip - ratio * row
        strip = strip * scale
        z_ref[top : top + BLOCK, :] = strip
        lt_ref[top : top + BLOCK, :] = strip[:, :KW]
        if top + BLOCK < KW:
            update = lax.dot_general(
                strip[:, :KW], strip, (((0,), (0,)), ((), ())), precision=HI,
                preferred_element_type=F32,
            )
            z_ref[top + BLOCK :, :] = z_ref[top + BLOCK :, :] - update[top + BLOCK :, :]


def factor_kernel(
    count, width, place_ref, s_ref, high_ref, low_ref, diag_ref, z_ref, lt_ref, mix_ref
):
    row_count, height = s_ref.shape[0], s_ref.shape[1]
    for p in range(row_count):
        interleave(mix_ref, p, row_count, s_ref[p])
    place = slot_place(count, width, place_ref[1])
    s = jnp.dot(whole_rows(mix_ref), place, precision=HI, preferred_element_type=F32)
    r = iota((KW, KW), 0)
    c = iota((KW, KW), 1)
    z_ref[:, :KW] = jnp.where(r >= c, s, 0.0) + jnp.where(r > c, s, 0.0).T
    z_ref[:, KW:] = (r == c).astype(F32)
    eliminate(z_ref, lt_ref)
    contract_last = (((1,), (1,)), ((), ()))
    inverse = jnp.where(r >= c, z_ref[:, KW:], 0.0)
    weights = lax.dot_general(
        place, inverse, contract_last, precision=HI, preferred_element_type=F32
    )
    high_ref[...], low_ref[...] = split(weights)
    upper = jnp.where(r <= c, lt_ref[...], 0.0)
    pick = iota((height, KW), 1) == iota((height, KW), 0) * row_count + place_ref[0]
    diag_ref[...] = lax.dot_general(
        pick.astype(F32), upper, contract_last, precision=HI, preferred_element_type=F32
    )


def whole(*shape):
    return pl.BlockSpec(shape, lambda i, place: (0,) * len(shape))


def factor_call(place, gathered, count, width):
    row_count, height = gathered.shape[0], gathered.shape[1]
    return pl.pallas_call(
        functools.partial(factor_kernel, count, width),
        grid_spec=pltpu.PrefetchScalarGridSpec(
            num_scalar_prefetch=1,
            grid=(1,),
            in_specs=[whole(row_count, height, KW)],
            out_specs=[whole(KW, KW), whole(KW, KW), whole(height, KW)],
            scratch_shapes=[
                pltpu.VMEM((KW, 2 * KW), F32),
                pltpu.VMEM((KW, KW), F32),
                pltpu.VMEM((KW // LANES, KW, LANES), F32),
            ],
        ),
        out_shape=[
            jax.ShapeDtypeStruct((KW, KW), BF16),
            jax.ShapeDtypeStruct((KW, KW), BF16),
            jax.ShapeDtypeStruct((height, KW), F32),
        ],
        compiler_params=PARAMS,
        cost_estimate=LIGHT,
        name="factor",
    )(place, gathered)


def columns_kernel(count, width, place_ref, head_ref, nh_ref, nl_ref, high_ref, low_ref, scr_ref):
    groups = head_ref.shape[0]
    tiles = head_ref.shape[2]
    height = head_ref.shape[3] * (LANES // width)
    for a in range(groups):
        for t in range(tiles):
            raw = unpack([head_ref[a, s, t] for s in range(count)], width)
            panel = dot3(raw, nh_ref[...], nl_ref[...])
            interleave(scr_ref, t * height * groups + a, groups, panel)
    cols = scr_ref.shape[1]
    l = iota((cols, KW), 0)
    c = iota((cols, KW), 1)
    pick = jnp.where(c == l * count + place_ref[1], -1.0, 0.0)
    weights = jnp.where(l < width, pick, whole_rows(scr_ref)).T
    high_ref[...], low_ref[...] = split(weights)


def columns_call(place, head, n_high, n_low, count, width, cols):
    return pl.pallas_call(
        functools.partial(columns_kernel, count, width),
        grid_spec=pltpu.PrefetchScalarGridSpec(
            num_scalar_prefetch=1,
            grid=(1,),
            in_specs=[whole(*head.shape), whole(KW, KW), whole(KW, KW)],
            out_specs=[whole(KW, cols), whole(KW, cols)],
            scratch_shapes=[pltpu.VMEM((KW // LANES, cols, LANES), F32)],
        ),
        out_shape=[jax.ShapeDtypeStruct((KW, cols), BF16)] * 2,
        compiler_params=PARAMS,
        cost_estimate=LIGHT,
        name="columns",
    )(place, head, n_high, n_low)


def update_kernel(count, width, row_count, first, skip, rows, tile, place_ref, *refs):
    ins = len(refs) - 10 - (first > 0)
    slots_in = refs[:ins]
    nh_ref, nl_ref, wh_ref, wl_ref, diag_ref, win_ref = refs[ins : ins + 6]
    out_ref, ring_ref, in_sem, out_sem = refs[-4:]
    p, q = place_ref[0], place_ref[1]
    groups = wh_ref.shape[1] // LANES
    part = tile // (LANES // width)
    steps = rows // tile
    depth = ring_ref.shape[0]
    ahead = steps if steps <= depth else depth // 2
    height = tile * groups
    dot = functools.partial(jnp.dot, preferred_element_type=F32)

    def place_of(i):
        return pl.ds(pl.multiple_of(first * groups + i * height, height), height)

    def fetch(i):
        slot = lax.rem(i, depth)
        return pltpu.make_async_copy(win_ref.at[place_of(i), :], ring_ref.at[slot], in_sem.at[slot])

    def store(i):
        slot = lax.rem(i, depth)
        return pltpu.make_async_copy(ring_ref.at[slot], out_ref.at[place_of(i), :], out_sem.at[slot])

    for i in range(ahead):
        fetch(jnp.int32(i)).start()

    def step(i, carry):
        span = pl.ds(pl.multiple_of(skip // (LANES // width) + i * part, part), part)
        slots = [slots_in[s][span, :] for s in range(count)]
        if ins > count:
            forwarded = slots_in[count][span, :]
            slots[1] = jnp.where(q == 0, forwarded, slots[1])
            slots[count - 1] = jnp.where(q == count - 1, forwarded, slots[count - 1])
        panel = dot3(unpack(slots, width), nh_ref[...], nl_ref[...])
        lane = iota((tile, LANES), 1)
        if first == 0:
            tall = diag_ref.shape[0]
            top = jnp.where(i == 0, diag_ref[...], panel[:tall])
            panel = jnp.concatenate([top, panel[tall:]], 0)
            global_row = (iota((tile, LANES), 0) + i * tile) * row_count + p
        high, low = split(panel)
        fetch(i).wait()
        buf = ring_ref.at[lax.rem(i, depth)]
        for pair in range(groups // 2):
            cols = slice(pair * 2 * LANES, (pair + 1) * 2 * LANES)
            w_high, w_low = wh_ref[:, cols], wl_ref[:, cols]
            update = dot(high, w_high) + (dot(high, w_low) + dot(low, w_high))
            for half in range(2):
                g = pair * 2 + half
                old = buf[pl.ds(g, tile, stride=groups), :]
                if g * LANES < width:
                    old = jnp.where(lane < width - g * LANES, 0.0, old)
                new = old - update[:, half * LANES : (half + 1) * LANES]
                if first == 0:
                    global_col = (lane + g * LANES) * count + q
                    new = jnp.where(global_row >= global_col, new, 0.0)
                buf[pl.ds(g, tile, stride=groups), :] = new
        store(i).start()

        @pl.when(i + ahead < steps)
        def _():
            @pl.when(i + ahead >= depth)
            def _():
                store(i + ahead - depth).wait()

            fetch(i + ahead).start()

        return carry

    lax.fori_loop(0, steps, step, 0)

    def drain(i, carry):
        store(i).wait()
        return carry

    lax.fori_loop(max(0, steps - depth), steps, drain, 0)


def update_call(
    place, chunk, weights, flat, out, first, skip, rows, tile, count, width, row_count
):
    groups = weights[2].shape[1] // LANES
    held = pl.BlockSpec(memory_space=pltpu.VMEM)
    far = pl.BlockSpec(memory_space=pl.ANY)
    specs = [held] * (len(chunk) + len(weights)) + [far]
    operands = [*chunk, *weights, flat]
    aliases = {}
    if out is not None:
        specs.append(far)
        operands.append(out)
        aliases = {len(operands): 0}
    depth = min(DEPTH, rows // tile)
    return pl.pallas_call(
        functools.partial(update_kernel, count, width, row_count, first, skip, rows, tile),
        grid_spec=pltpu.PrefetchScalarGridSpec(
            num_scalar_prefetch=1,
            grid=(1,),
            in_specs=specs,
            out_specs=far,
            scratch_shapes=[
                pltpu.VMEM((depth, tile * groups, LANES), F32),
                pltpu.SemaphoreType.DMA((depth,)),
                pltpu.SemaphoreType.DMA((depth,)),
            ],
        ),
        out_shape=jax.ShapeDtypeStruct(flat.shape, F32),
        input_output_aliases=aliases,
        compiler_params=PARAMS,
        cost_estimate=pl.CostEstimate(
            flops=6 * rows * KW * (KW + groups * LANES),
            bytes_accessed=rows * 4 * (2 * groups * LANES + KW),
            transcendentals=0,
        ),
        name="update",
    )(place, *operands)


def chunk_sizes(units):
    sizes = [1]
    for share in SHARES:
        sizes.append(max(1, units * share // 16))
    return sizes + [units - sum(sizes)]


def body(window):
    local_rows = window.shape[1]
    local_cols = window.shape[3]
    row_count = lax.axis_size("row")
    count = lax.axis_size("col")
    p = lax.axis_index("row")
    q = lax.axis_index("col")
    width = KW // count
    height = KW // row_count
    head_rows = local_cols * count // row_count
    groups = row_count // count
    tile = min(TILE, head_rows)
    place = jnp.stack([p, q]).astype(jnp.int32)
    flat = window.reshape(local_rows * local_cols // LANES, LANES)

    sizes = [x * tile for x in chunk_sizes(local_rows // tile)]
    starts = [sum(sizes[:i]) for i in range(len(sizes))]
    packed = [pack_rows(window, f, r, tile, width) for f, r in zip(starts, sizes)]

    def shift(x, k):
        return lax.ppermute(x, "col", [(i, (i + k) % count) for i in range(count)])

    fold = LANES // width
    slots = [[packed[0]] + [shift(packed[0], k) for k in range(1, count)]]
    early = tuple(packed[1:3])
    slots[0] = list(lax.optimization_barrier((*slots[0], *early)))[:count]
    head = jnp.stack(slots[0])

    lead = head[:, :height, :width]
    lead = lead.transpose(1, 0, 2).reshape(height, KW)
    gathered = lax.all_gather(lead, "row")
    n_high, n_low, diag = factor_call(place, gathered, count, width)

    spread = head
    bit = 1
    while bit < count:
        pairs = [(i, i ^ bit) for i in range(row_count)]
        other = lax.ppermute(spread, "row", pairs)
        spread = jnp.where(((p ^ q) & bit) != 0, other, spread)
        bit *= 2
    spread = spread[None]
    while bit < row_count:
        pairs = [(i, i ^ bit) for i in range(row_count)]
        other = lax.ppermute(spread, "row", pairs)
        low = (p & bit) == 0
        spread = jnp.concatenate(
            [jnp.where(low, spread, other), jnp.where(low, other, spread)], 0
        )
        bit *= 2
    spread = spread.reshape(groups, count, head_rows // tile, tile // fold, LANES)

    def update(j, out, skip=0, rows=None):
        rows = sizes[j] - skip if rows is None else rows
        return update_call(
            place, slots[j], weights, flat, out, starts[j] + skip, skip, rows, tile,
            count, width, row_count,
        )

    after = lambda x, *others: lax.optimization_barrier((x, *others))[0]

    if count != 4:
        slots += [[x] + [shift(x, k) for k in range(1, count)] for x in packed[1:]]
        made = columns_call(place, spread, n_high, n_low, count, width, local_cols)
        weights = [n_high, n_low, *made, diag]
        out = None
        for j in range(len(sizes)):
            out = update(j, out)
        return out.reshape(window.shape)

    up = [(0, 1), (1, 2), (2, 3)]
    down = [(1, 0), (2, 1), (3, 2)]
    outward = [(2, 3), (1, 0)]
    send = lambda x, pairs: lax.ppermute(x, "col", pairs)

    def forward(j, *others):
        slots[j].append(send(after(slots[j][2], *others), outward))

    x = packed[1]
    slots.append([x, send(x, up), shift(x, 2), send(x, down)])
    two = shift(packed[2], 2)
    forward(1, n_high)
    made = columns_call(place, spread, n_high, n_low, count, width, local_cols)
    weights = [n_high, n_low, *made, diag]
    out = update(0, None)
    x, third, out, *_ = lax.optimization_barrier(
        (packed[2], packed[3], out, slots[1][1], slots[1][3])
    )
    slots.append([x, send(x, up), two, send(x, down)])
    part = -(-sizes[1] // tile // 2) * tile
    out = update(1, out, rows=part)
    slots[2][2], third, out = lax.optimization_barrier((slots[2][2], third, out))
    forward(2)
    slots.append([third, send(third, up), shift(third, 2), send(third, down)])
    out = update(1, out, skip=part)
    slots[3][2], out = lax.optimization_barrier((slots[3][2], out))
    forward(3)
    out = update(2, out)
    out = update(3, out)
    return out.reshape(window.shape)


def solution(mesh):
    spec = P("row", None, "col", None)
    return jax.shard_map(body, mesh=mesh, in_specs=(spec,), out_specs=spec, check_vma=False)
```

time: 208 us -> 168 us (0.81)
  starting transfers between devices: 68.7 us -> 38.3 us
  waiting for transfers between devices: 26.9 us -> 22 us
  local copies, waits for them, and re-layouts: 7.63 us -> 3.37 us
  Pallas kernels: 85.7 us -> 88 us
    ppermute x24 -> x15, starting transfers between devices: 65.7 us -> 35.3 us  [the longest x9 30.8 us: body(): send = lambda x, pairs: lax.ppermute(x, 'col', pairs)]
    ppermute x24 -> x15, waiting for transfers between devices: 26.9 us -> 10.4 us  [the longest x9 6.53 us: body(): send = lambda x, pairs: lax.ppermute(x, 'col', pairs)]
    ppermute x3, waiting for transfers between devices: 0.01 us -> 11.5 us  [body(): other = lax.ppermute(spread, 'row', pairs)]
    pallas_call x4 -> x5, Pallas kernels: 45.5 us -> 48.6 us  [update_call(): pl.pallas_call(functools.partial(update_kernel, count, width, row_count,...]
    unnamed x30 -> x14, local copies, waits for them, and re-layouts: 4.55 us -> 2.37 us
  transfers between devices with their start and end apart: 27 -> 18, of which waited for: 9 -> 6; matrix products, arithmetic and copies ran while one was open for 4% -> 3% of each run, Pallas kernels for 35% -> 48%
where the time goes in v1:
time: 168 us; the launch traced here: 167 us
  Pallas kernels  88 us (52%)
  starting transfers between devices  38.3 us (23%)
  waiting for transfers between devices  22 us (13%)
  blocking collectives  9.52 us (6%)
  other arithmetic  5.05 us (3%)
  local copies, waits for them, and re-layouts  3.37 us (2%)
    pallas_call x5, Pallas kernels, update_call(): pl.pallas_call(functools.partial(update_kernel, count, width, row_count,...  48.6 us
    ppermute x9, starting transfers between devices, body(): send = lambda x, pairs: lax.ppermute(x, 'col', pairs)  30.8 us
    pallas_call x1, Pallas kernels, factor_call(): pl.pallas_call(functools.partial(factor_kernel, count, width), grid_spec=...  27.8 us
    ppermute x3, waiting for transfers between devices, body(): other = lax.ppermute(spread, 'row', pairs)  11.5 us
    pallas_call x4, Pallas kernels, pack_rows(): pl.pallas_call(functools.partial(pack_kernel, width), grid=(rows // tile,...  10.1 us
    all_gather x1, blocking collectives, body(): gathered = lax.all_gather(lead, 'row')  9.52 us
    ppermute x9, waiting for transfers between devices, body(): send = lambda x, pairs: lax.ppermute(x, 'col', pairs)  6.53 us
    ppermute x6, starting transfers between devices, shift(): return lax.ppermute(x, 'col', [(i, (i + k) % count) for i in range(count)])  4.48 us
  transfers between devices with their start and end apart: 18, of which 6 were waited for; matrix products, arithmetic and copies ran while one was open for 3% of the time, Pallas kernels for 48%

profile of v1, /device:TPU:16, one launch (start us, length us, event | category | flops | bytes accessed | tf_op | source)
XLA Modules:
  0.0 166.7 jit_solution(14765126814181795532)
XLA Ops:
  0.0 1.1 pack.6.refs_0_
  1.1 1.6 collective-permute-start.1
  3.0 1.2 collective-permute-start.3
  4.3 5.5 %pack.7.refs_0_ = f32[2304,128]{1,0:T(8,128)S(1)} custom-call(f32[1,8192,1,1024]{3,2,1,0:T(1,128)} %win_ref.7), custom_call_target="tpu_custom_call" | custom-call | tf_op jit(solution)/shard_map/pack/pallas_call | solution.py:55
  9.7 2.4 %pack.4.refs_0_ = f32[1024,128]{1,0:T(8,128)S(1)} custom-call(f32[1,8192,1,1024]{3,2,1,0:T(1,128)} %win_ref.7), custom_call_target="tpu_custom_call" | custom-call | tf_op jit(solution)/shard_map/pack/pallas_call | solution.py:55
  12.1 1.0 collective-permute-done.1.refs_1_
  14.5 1.2 collective-permute-start.9
  17.6 1.5 collective-permute-start.5
  19.1 5.6 %collective-permute-start.7 = (f32[2304,128]{1,0:T(8,128)S(1)}, f32[2304,128]{1,0:T(8,128)}, u32[]{:S(2)}, u32[]{:S(2)}) collective-permute-start(f32[2304,128]{1,0:T(8,128)S(1)} %pack.7.refs_0_), channel_id=1, source_target_pairs={{0,1},{1,2},{2,3},{4,5},{5,6},{6,7},{8,9},{9,10},{10,11},{12,13},{... | collective-permute-start | bytes 3538952 | tf_op jit(solution)/shard_map/ppermute | solution.py:415
  24.7 1.9 %collective-permute-start.8 = (f32[2304,128]{1,0:T(8,128)S(1)}, f32[2304,128]{1,0:T(8,128)}, u32[]{:S(2)}, u32[]{:S(2)}) collective-permute-start(f32[2304,128]{1,0:T(8,128)S(1)} %pack.7.refs_0_), channel_id=1, source_target_pairs={{1,0},{2,1},{3,2},{5,4},{6,5},{7,6},{9,8},{10,9},{11,10},{13,12},{... | collective-permute-start | bytes 3538952 | tf_op jit(solution)/shard_map/ppermute | solution.py:415
  27.7 9.5 %all_gather.3.s_ref = f32[8,32,256]{2,1,0:T(8,128)S(1)} all-gather(f32[1,32,256]{2,1,0:T(8,128)S(1)} %all_gather_reshape.3), channel_id=1, replica_groups=mesh['row'=8,'col'=4] {'row'}, dimensions={0}, use_global_device_ids=true | all-gather | bytes 294912 | tf_op jit(solution)/shard_map/all_gather | solution.py:373
  37.2 27.8 %factor.1 = (bf16[256,256]{1,0:T(8,128)(2,1)S(1)}, bf16[256,256]{1,0:T(8,128)(2,1)S(1)}, f32[32,256]{1,0:T(8,128)S(1)}) custom-call(s32[2]{0:T(128)S(1)} %pad_add_fusion.place_ref, f32[8,32,256]{2,1,0:T(8,128)S(1)} %all_gather.3.s_ref), custom_call_target="tpu_custom_call" | custom-call | tf_op jit(solution)/shard_map/factor/pallas_call | solution.py:159
  65.0 2.4 %collective-permute-done.9.refs_2_ = f32[2304,128]{1,0:T(8,128)S(1)} collective-permute-done((f32[2304,128]{1,0:T(8,128)S(1)}, f32[2304,128]{1,0:T(8,128)S(1)}, u32[]{:S(2)}, u32[]{:S(2)}) %collective-permute-start.9) | collective-permute-done | bytes 1179680 | tf_op jit(solution)/shard_map/ppermute | solution.py:363
  67.3 6.2 %collective-permute-start.10 = (f32[2304,128]{1,0:T(8,128)S(1)}, f32[2304,128]{1,0:T(8,128)}, u32[]{:S(2)}, u32[]{:S(2)}) collective-permute-start(f32[2304,128]{1,0:T(8,128)S(1)} %collective-permute-done.9.refs_2_), channel_id=1, source_target_pairs={{2,3},{1,0},{6,7},{5,4},{10,11},{9,8},{14,15},{13,12},{18,19},{17,... | collective-permute-start | bytes 3538952 | tf_op jit(solution)/shard_map/ppermute | solution.py:415
  73.5 1.9 %select_bitcast_fusion = f32[1,4,256,128]{3,2,1,0:T(8,128)} fusion(f32[4,256,128]{2,1,0:T(8,128)} %collective-permute-done.5, pred[]{:T(512)S(6)} %ne.6, f32[4,256,128]{2,1,0:T(8,128)} %collective-permute-done.4, f32[1,256,128]{2,1,0:T(8,128)} %bitcast.27, f32[1,256,128]{2,1,0:T(8,128)S(1)} %bitcast.24, f32[1,256,128]{2,1,0:T(8,128)S(1)} %bitcast.21, ...), kind=kLoop, calls=%fused_computation.2 | loop fusion | flops 655360 | bytes 2097154 | tf_op jit(solution)/shard_map/broadcast_in_dim | solution.py:383
  75.4 1.5 collective-permute-start.6
  77.0 1.2 pack.5.refs_0_
  78.9 10.5 %collective-permute-done.6 = f32[1,4,256,128]{3,2,1,0:T(8,128)} collective-permute-done((f32[1,4,256,128]{3,2,1,0:T(8,128)}, f32[1,4,256,128]{3,2,1,0:T(8,128)}, u32[]{:S(2)}, u32[]{:S(2)}) %collective-permute-start.6) | collective-permute-done | bytes 524320 | tf_op jit(solution)/shard_map/ppermute | solution.py:386
  89.5 1.3 broadcast_select_fusion.2
  90.8 1.5 columns.1
  94.0 5.2 %update.5.refs_11_ = f32[65536,128]{1,0:T(8,128)} custom-call(s32[2]{0:T(128)S(1)} %pad_add_fusion.place_ref, f32[256,128]{1,0:T(8,128)S(1)} %pack.6.refs_0_, f32[256,128]{1,0:T(8,128)S(1)} %collective-permute-done.1.refs_1_, f32[256,128]{1,0:T(8,128)S(1)} %collective-permute-done.2.refs_2_, f32[256,128]{1,0:T(8,128)S(1)} %copy-done.1, ...), custom_call_target="tpu_custom_call" | custom-call | flops 1006632960 | bytes 4718592 | tf_op jit(solution)/shard_map/update/pallas_call | solution.py:311
  99.2 6.5 %collective-permute-done.7.refs_1_ = f32[2304,128]{1,0:T(8,128)} collective-permute-done((f32[2304,128]{1,0:T(8,128)S(1)}, f32[2304,128]{1,0:T(8,128)}, u32[]{:S(2)}, u32[]{:S(2)}) %collective-permute-start.7) | collective-permute-done | bytes 1179680 | tf_op jit(solution)/shard_map/ppermute | solution.py:415
  105.7 1.9 %collective-permute-start.15 = (f32[1024,128]{1,0:T(8,128)S(1)}, f32[1024,128]{1,0:T(8,128)S(1)}, u32[]{:S(2)}, u32[]{:S(2)}) collective-permute-start(f32[1024,128]{1,0:T(8,128)S(1)} %pack.4.refs_0_), channel_id=1, source_target_pairs={{0,1},{1,2},{2,3},{4,5},{5,6},{6,7},{8,9},{9,10},{10,11},{12,13},{... | collective-permute-start | bytes 1572872 | tf_op jit(solution)/shard_map/ppermute | solution.py:415
  107.6 3.9 %collective-permute-start.16 = (f32[1024,128]{1,0:T(8,128)S(1)}, f32[1024,128]{1,0:T(8,128)S(1)}, u32[]{:S(2)}, u32[]{:S(2)}) collective-permute-start(f32[1024,128]{1,0:T(8,128)S(1)} %pack.4.refs_0_), channel_id=1, source_target_pairs={{1,0},{2,1},{3,2},{5,4},{6,5},{7,6},{9,8},{10,9},{11,10},{13,12},{... | collective-permute-start | bytes 1572872 | tf_op jit(solution)/shard_map/ppermute | solution.py:415
  111.6 13.8 %update.6.refs_11_ = f32[65536,128]{1,0:T(8,128)} custom-call(s32[2]{0:T(128)S(1)} %pad_add_fusion.place_ref, f32[2304,128]{1,0:T(8,128)S(1)} %pack.7.refs_0_, f32[2304,128]{1,0:T(8,128)} %collective-permute-done.7.refs_1_, f32[2304,128]{1,0:T(8,128)S(1)} %collective-permute-done.9.refs_2_, ...), custom_call_target="tpu_custom_call", output_to_operand_aliasing={{}: (12, {})} | custom-call | flops 5033164800 | bytes 23592960 | tf_op jit(solution)/shard_map/update/pallas_call | solution.py:311
  125.4 2.0 %collective-permute-start.17 = (f32[1024,128]{1,0:T(8,128)}, f32[1024,128]{1,0:T(8,128)S(1)}, u32[]{:S(2)}, u32[]{:S(2)}) collective-permute-start(f32[1024,128]{1,0:T(8,128)} %collective-permute-done.refs_2_), channel_id=1, source_target_pairs={{2,3},{1,0},{6,7},{5,4},{10,11},{9,8},{14,15},{13,12},{18,19},{17,... | collective-permute-start | bytes 1572872 | tf_op jit(solution)/shard_map/ppermute | solution.py:415
  127.5 3.4 %collective-permute-start.11 = (f32[512,128]{1,0:T(8,128)S(1)}, f32[512,128]{1,0:T(8,128)S(1)}, u32[]{:S(2)}, u32[]{:S(2)}) collective-permute-start(f32[512,128]{1,0:T(8,128)S(1)} %copy-done.3), channel_id=1, source_target_pairs={{0,1},{1,2},{2,3},{4,5},{5,6},{6,7},{8,9},{9,10},{10,11},{12,13},{... | collective-permute-start | bytes 786440 | tf_op jit(solution)/shard_map/ppermute | solution.py:415
  130.9 12.0 %update.7.refs_11_ = f32[65536,128]{1,0:T(8,128)} custom-call(s32[2]{0:T(128)S(1)} %pad_add_fusion.place_ref, f32[2304,128]{1,0:T(8,128)S(1)} %pack.7.refs_0_, f32[2304,128]{1,0:T(8,128)} %collective-permute-done.7.refs_1_, f32[2304,128]{1,0:T(8,128)S(1)} %collective-permute-done.9.refs_2_, ...), custom_call_target="tpu_custom_call", output_to_operand_aliasing={{}: (12, {})} | custom-call | flops 4026531840 | bytes 18874368 | tf_op jit(solution)/shard_map/update/pallas_call | solution.py:311
  143.0 2.4 %collective-permute-start.13 = (f32[512,128]{1,0:T(8,128)S(1)}, f32[512,128]{1,0:T(8,128)S(1)}, u32[]{:S(2)}, u32[]{:S(2)}) collective-permute-start(f32[512,128]{1,0:T(8,128)S(1)} %copy-done.3), channel_id=1, source_target_pairs={{1,0},{2,1},{3,2},{5,4},{6,5},{7,6},{9,8},{10,9},{11,10},{13,12},{... | collective-permute-start | bytes 786440 | tf_op jit(solution)/shard_map/ppermute | solution.py:415
  145.4 3.4 %collective-permute-start.14 = (f32[512,128]{1,0:T(8,128)S(1)}, f32[512,128]{1,0:T(8,128)S(1)}, u32[]{:S(2)}, u32[]{:S(2)}) collective-permute-start(f32[512,128]{1,0:T(8,128)S(1)} %collective-permute-done.12.refs_2_), channel_id=1, source_target_pairs={{2,3},{1,0},{6,7},{5,4},{10,11},{9,8},{14,15},{13,12},{18,19},{17,... | collective-permute-start | bytes 786440 | tf_op jit(solution)/shard_map/ppermute | solution.py:415
  148.9 11.1 %update.8.refs_11_ = f32[65536,128]{1,0:T(8,128)} custom-call(s32[2]{0:T(128)S(1)} %pad_add_fusion.place_ref, f32[1024,128]{1,0:T(8,128)S(1)} %pack.4.refs_0_, f32[1024,128]{1,0:T(8,128)S(1)} %collective-permute-done.15.refs_1_, f32[1024,128]{1,0:T(8,128)} %collective-permute-done.refs_2_, ...), custom_call_target="tpu_custom_call", output_to_operand_aliasing={{}: (12, {})} | custom-call | flops 4026531840 | bytes 18874368 | tf_op jit(solution)/shard_map/update/pallas_call | solution.py:311
  160.0 6.5 %update.9 = f32[65536,128]{1,0:T(8,128)} custom-call(s32[2]{0:T(128)S(1)} %pad_add_fusion.place_ref, f32[512,128]{1,0:T(8,128)S(1)} %copy-done.3, f32[512,128]{1,0:T(8,128)S(1)} %collective-permute-done.11.refs_1_, f32[512,128]{1,0:T(8,128)S(1)} %collective-permute-done.12.refs_2_, ...), custom_call_target="tpu_custom_call", output_to_operand_aliasing={{}: (12, {})} | custom-call | flops 2013265920 | bytes 9437184 | tf_op jit(solution)/shard_map/update/pallas_call | solution.py:311
  (39 shorter events, 7.1 us)
Async XLA Ops:
  1.1 12.1 %collective-permute-start.1 = (f32[256,128]{1,0:T(8,128)S(1)}, f32[256,128]{1,0:T(8,128)S(1)}, u32[]{:S(2)}, u32[]{:S(2)}) collective-permute-start(f32[256,128]{1,0:T(8,128)S(1)} %pack.6.refs_0_), channel_id=1, source_target_pairs={{0,1},{1,2},{2,3},{3,0},{4,5},{5,6},{6,7},{7,4},{8,9},{9,10},{10,1... | collective-permute-start | bytes 393224 | tf_op jit(solution)/shard_map/ppermute | solution.py:363
  2.7 10.4 %collective-permute-start.2 = (f32[256,128]{1,0:T(8,128)S(1)}, f32[256,128]{1,0:T(8,128)S(1)}, u32[]{:S(2)}, u32[]{:S(2)}) collective-permute-start(f32[256,128]{1,0:T(8,128)S(1)} %pack.6.refs_0_), channel_id=1, source_target_pairs={{0,2},{1,3},{2,0},{3,1},{4,6},{5,7},{6,4},{7,5},{8,10},{9,11},{10,... | collective-permute-start | bytes 393224 | tf_op jit(solution)/shard_map/ppermute | solution.py:363
  3.0 10.6 %collective-permute-start.3 = (f32[256,128]{1,0:T(8,128)S(1)}, f32[256,128]{1,0:T(8,128)S(1)}, u32[]{:S(2)}, u32[]{:S(2)}) collective-permute-start(f32[256,128]{1,0:T(8,128)S(1)} %pack.6.refs_0_), channel_id=1, source_target_pairs={{0,3},{1,0},{2,1},{3,2},{4,7},{5,4},{6,5},{7,6},{8,11},{9,8},{10,9... | collective-permute-start | bytes 393224 | tf_op jit(solution)/shard_map/ppermute | solution.py:363
  13.6 14.0 %copy-start = (f32[256,128]{1,0:T(8,128)}, f32[256,128]{1,0:T(8,128)S(1)}, u32[]{:S(2)}) copy-start(f32[256,128]{1,0:T(8,128)S(1)} %collective-permute-done.3.refs_3_) | copy-start | bytes 393220
  14.5 2.3 %collective-permute-start.4 = (f32[4,256,128]{2,1,0:T(8,128)}, f32[4,256,128]{2,1,0:T(8,128)}, u32[]{:S(2)}, u32[]{:S(2)}) collective-permute-start(f32[4,256,128]{2,1,0:T(8,128)} %pad_maximum_fusion), channel_id=1, source_target_pairs={{0,4},{4,0},{8,12},{12,8},{16,20},{20,16},{24,28},{28,24},{1,5},{5... | collective-permute-start | bytes 1572872 | tf_op jit(solution)/shard_map/ppermute | solution.py:380
  14.5 52.8 %collective-permute-start.9 = (f32[2304,128]{1,0:T(8,128)S(1)}, f32[2304,128]{1,0:T(8,128)S(1)}, u32[]{:S(2)}, u32[]{:S(2)}) collective-permute-start(f32[2304,128]{1,0:T(8,128)S(1)} %pack.7.refs_0_), channel_id=1, source_target_pairs={{0,2},{1,3},{2,0},{3,1},{4,6},{5,7},{6,4},{7,5},{8,10},{9,11},{10,... | collective-permute-start | bytes 3538952 | tf_op jit(solution)/shard_map/ppermute | solution.py:363
  17.6 55.9 %collective-permute-start.5 = (f32[4,256,128]{2,1,0:T(8,128)}, f32[4,256,128]{2,1,0:T(8,128)}, u32[]{:S(2)}, u32[]{:S(2)}) collective-permute-start(f32[4,256,128]{2,1,0:T(8,128)} %broadcast_select_fusion), channel_id=1, source_target_pairs={{0,8},{4,12},{8,0},{12,4},{16,24},{20,28},{24,16},{28,20},{1,9},{5... | collective-permute-start | bytes 1572872 | tf_op jit(solution)/shard_map/ppermute | solution.py:380
  19.1 86.7 %collective-permute-start.7 = (f32[2304,128]{1,0:T(8,128)S(1)}, f32[2304,128]{1,0:T(8,128)}, u32[]{:S(2)}, u32[]{:S(2)}) collective-permute-start(f32[2304,128]{1,0:T(8,128)S(1)} %pack.7.refs_0_), channel_id=1, source_target_pairs={{0,1},{1,2},{2,3},{4,5},{5,6},{6,7},{8,9},{9,10},{10,11},{12,13},{... | collective-permute-start | bytes 3538952 | tf_op jit(solution)/shard_map/ppermute | solution.py:415
  24.7 81.1 %collective-permute-start.8 = (f32[2304,128]{1,0:T(8,128)S(1)}, f32[2304,128]{1,0:T(8,128)}, u32[]{:S(2)}, u32[]{:S(2)}) collective-permute-start(f32[2304,128]{1,0:T(8,128)S(1)} %pack.7.refs_0_), channel_id=1, source_target_pairs={{1,0},{2,1},{3,2},{5,4},{6,5},{7,6},{9,8},{10,9},{11,10},{13,12},{... | collective-permute-start | bytes 3538952 | tf_op jit(solution)/shard_map/ppermute | solution.py:415
  64.9 12.0 %copy-start.4 = (f32[32,256]{1,0:T(8,128)}, f32[32,256]{1,0:T(8,128)S(1)}, u32[]{:S(2)}) copy-start(f32[32,256]{1,0:T(8,128)S(1)} %get-tuple-element.31.refs_8_.refs_9_) | copy-start | bytes 98308
  67.3 44.3 %collective-permute-start.10 = (f32[2304,128]{1,0:T(8,128)S(1)}, f32[2304,128]{1,0:T(8,128)}, u32[]{:S(2)}, u32[]{:S(2)}) collective-permute-start(f32[2304,128]{1,0:T(8,128)S(1)} %collective-permute-done.9.refs_2_), channel_id=1, source_target_pairs={{2,3},{1,0},{6,7},{5,4},{10,11},{9,8},{14,15},{13,12},{18,19},{17,... | collective-permute-start | bytes 3538952 | tf_op jit(solution)/shard_map/ppermute | solution.py:415
  75.4 14.0 %collective-permute-start.6 = (f32[1,4,256,128]{3,2,1,0:T(8,128)}, f32[1,4,256,128]{3,2,1,0:T(8,128)}, u32[]{:S(2)}, u32[]{:S(2)}) collective-permute-start(f32[1,4,256,128]{3,2,1,0:T(8,128)} %select_bitcast_fusion), channel_id=1, source_target_pairs={{0,16},{4,20},{8,24},{12,28},{16,0},{20,4},{24,8},{28,12},{1,17},{... | collective-permute-start | bytes 1572872 | tf_op jit(solution)/shard_map/ppermute | solution.py:386
  77.0 48.4 %collective-permute-start = (f32[1024,128]{1,0:T(8,128)S(1)}, f32[1024,128]{1,0:T(8,128)}, u32[]{:S(2)}, u32[]{:S(2)}) collective-permute-start(f32[1024,128]{1,0:T(8,128)S(1)} %pack.4.refs_0_), channel_id=1, source_target_pairs={{0,2},{1,3},{2,0},{3,1},{4,6},{5,7},{6,4},{7,5},{8,10},{9,11},{10,... | collective-permute-start | bytes 1572872 | tf_op jit(solution)/shard_map/ppermute | solution.py:363
  78.2 0.7 copy-start.2
  92.4 0.9 copy-start.1
  93.3 0.8 copy-start.5
  94.0 17.6 %copy-start.6 = (f32[32,256]{1,0:T(8,128)S(1)}, f32[32,256]{1,0:T(8,128)}, u32[]{:S(2)}) copy-start(f32[32,256]{1,0:T(8,128)} %copy-done.4) | copy-start | bytes 98308
  99.2 28.2 %copy-start.3 = (f32[512,128]{1,0:T(8,128)S(1)}, f32[512,128]{1,0:T(8,128)}, u32[]{:S(2)}) copy-start(f32[512,128]{1,0:T(8,128)} %copy-done.2) | copy-start | bytes 786436
  105.7 39.7 %collective-permute-start.15 = (f32[1024,128]{1,0:T(8,128)S(1)}, f32[1024,128]{1,0:T(8,128)S(1)}, u32[]{:S(2)}, u32[]{:S(2)}) collective-permute-start(f32[1024,128]{1,0:T(8,128)S(1)} %pack.4.refs_0_), channel_id=1, source_target_pairs={{0,1},{1,2},{2,3},{4,5},{5,6},{6,7},{8,9},{9,10},{10,11},{12,13},{... | collective-permute-start | bytes 1572872 | tf_op jit(solution)/shard_map/ppermute | solution.py:415
  107.6 41.2 %collective-permute-start.16 = (f32[1024,128]{1,0:T(8,128)S(1)}, f32[1024,128]{1,0:T(8,128)S(1)}, u32[]{:S(2)}, u32[]{:S(2)}) collective-permute-start(f32[1024,128]{1,0:T(8,128)S(1)} %pack.4.refs_0_), channel_id=1, source_target_pairs={{1,0},{2,1},{3,2},{5,4},{6,5},{7,6},{9,8},{10,9},{11,10},{13,12},{... | collective-permute-start | bytes 1572872 | tf_op jit(solution)/shard_map/ppermute | solution.py:415
  125.4 23.5 %collective-permute-start.17 = (f32[1024,128]{1,0:T(8,128)}, f32[1024,128]{1,0:T(8,128)S(1)}, u32[]{:S(2)}, u32[]{:S(2)}) collective-permute-start(f32[1024,128]{1,0:T(8,128)} %collective-permute-done.refs_2_), channel_id=1, source_target_pairs={{2,3},{1,0},{6,7},{5,4},{10,11},{9,8},{14,15},{13,12},{18,19},{17,... | collective-permute-start | bytes 1572872 | tf_op jit(solution)/shard_map/ppermute | solution.py:415
  127.4 15.5 %collective-permute-start.12 = (f32[512,128]{1,0:T(8,128)S(1)}, f32[512,128]{1,0:T(8,128)S(1)}, u32[]{:S(2)}, u32[]{:S(2)}) collective-permute-start(f32[512,128]{1,0:T(8,128)S(1)} %copy-done.3), channel_id=1, source_target_pairs={{0,2},{1,3},{2,0},{3,1},{4,6},{5,7},{6,4},{7,5},{8,10},{9,11},{10,... | collective-permute-start | bytes 786440 | tf_op jit(solution)/shard_map/ppermute | solution.py:363
  127.5 32.5 %collective-permute-start.11 = (f32[512,128]{1,0:T(8,128)S(1)}, f32[512,128]{1,0:T(8,128)S(1)}, u32[]{:S(2)}, u32[]{:S(2)}) collective-permute-start(f32[512,128]{1,0:T(8,128)S(1)} %copy-done.3), channel_id=1, source_target_pairs={{0,1},{1,2},{2,3},{4,5},{5,6},{6,7},{8,9},{9,10},{10,11},{12,13},{... | collective-permute-start | bytes 786440 | tf_op jit(solution)/shard_map/ppermute | solution.py:415
  143.0 17.0 %collective-permute-start.13 = (f32[512,128]{1,0:T(8,128)S(1)}, f32[512,128]{1,0:T(8,128)S(1)}, u32[]{:S(2)}, u32[]{:S(2)}) collective-permute-start(f32[512,128]{1,0:T(8,128)S(1)} %copy-done.3), channel_id=1, source_target_pairs={{1,0},{2,1},{3,2},{5,4},{6,5},{7,6},{9,8},{10,9},{11,10},{13,12},{... | collective-permute-start | bytes 786440 | tf_op jit(solution)/shard_map/ppermute | solution.py:415
  145.4 14.6 %collective-permute-start.14 = (f32[512,128]{1,0:T(8,128)S(1)}, f32[512,128]{1,0:T(8,128)S(1)}, u32[]{:S(2)}, u32[]{:S(2)}) collective-permute-start(f32[512,128]{1,0:T(8,128)S(1)} %collective-permute-done.12.refs_2_), channel_id=1, source_target_pairs={{2,3},{1,0},{6,7},{5,4},{10,11},{9,8},{14,15},{13,12},{18,19},{17,... | collective-permute-start | bytes 786440 | tf_op jit(solution)/shard_map/ppermute | solution.py:415

commit v2 on v1

--- a/solution.py
+++ b/solution.py
@@ -419,15 +419,14 @@
 
     x = packed[1]
     slots.append([x, send(x, up), shift(x, 2), send(x, down)])
-    two = shift(packed[2], 2)
     forward(1, n_high)
     made = columns_call(place, spread, n_high, n_low, count, width, local_cols)
     weights = [n_high, n_low, *made, diag]
     out = update(0, None)
-    x, third, out, *_ = lax.optimization_barrier(
-        (packed[2], packed[3], out, slots[1][1], slots[1][3])
+    x, third, slots[1][1], slots[1][3] = lax.optimization_barrier(
+        (packed[2], packed[3], slots[1][1], slots[1][3])
     )
-    slots.append([x, send(x, up), two, send(x, down)])
+    slots.append([x, send(x, up), shift(x, 2), send(x, down)])
     part = -(-sizes[1] // tile // 2) * tile
     out = update(1, out, rows=part)
     slots[2][2], third, out = lax.optimization_barrier((slots[2][2], third, out))

time: 168 us -> 167 us (level)
    ppermute x3, waiting for transfers between devices: 11.5 us -> 1.01 us  [body(): other = lax.ppermute(spread, 'row', pairs)]
    ppermute x9, waiting for transfers between devices: 6.53 us -> 15.5 us  [body(): send = lambda x, pairs: lax.ppermute(x, 'col', pairs)]
  transfers between devices with their start and end apart: 18 -> 18, of which waited for: 6 -> 5; matrix products, arithmetic and copies ran while one was open for 3% -> 3% of each run, Pallas kernels for 48% -> 48%
where the time goes in v2:
time: 167 us; the launch traced here: 165 us
  Pallas kernels  87 us (52%)
  starting transfers between devices  38.8 us (23%)
  waiting for transfers between devices  20.4 us (12%)
  blocking collectives  9.52 us (6%)
  other arithmetic  5.06 us (3%)
  local copies, waits for them, and re-layouts  3.37 us (2%)
    pallas_call x5, Pallas kernels, update_call(): pl.pallas_call(functools.partial(update_kernel, count, width, row_count,...  47.6 us
    ppermute x9, starting transfers between devices, body(): send = lambda x, pairs: lax.ppermute(x, 'col', pairs)  31.3 us
    pallas_call x1, Pallas kernels, factor_call(): pl.pallas_call(functools.partial(factor_kernel, count, width), grid_spec=...  27.8 us
    ppermute x9, waiting for transfers between devices, body(): send = lambda x, pairs: lax.ppermute(x, 'col', pairs)  15.5 us
    pallas_call x4, Pallas kernels, pack_rows(): pl.pallas_call(functools.partial(pack_kernel, width), grid=(rows // tile,...  10.1 us
    all_gather x1, blocking collectives, body(): gathered = lax.all_gather(lead, 'row')  9.52 us
    ppermute x6, starting transfers between devices, shift(): return lax.ppermute(x, 'col', [(i, (i + k) % count) for i in range(count)])  4.48 us
    ppermute x6, waiting for transfers between devices, shift(): return lax.ppermute(x, 'col', [(i, (i + k) % count) for i in range(count)])  3.89 us
  transfers between devices with their start and end apart: 18, of which 5 were waited for; matrix products, arithmetic and copies ran while one was open for 3% of the time, Pallas kernels for 48%

profile of v2, /device:TPU:16, one launch (start us, length us, event | category | flops | bytes accessed | tf_op | source)
XLA Modules:
  0.0 164.6 jit_solution(4864296265354018359)
XLA Ops:
  0.0 1.1 pack.7.refs_0_
  1.1 1.6 collective-permute-start.4
  3.0 1.2 collective-permute-start.6
  4.3 5.5 %pack.6.refs_0_ = f32[2304,128]{1,0:T(8,128)S(1)} custom-call(f32[1,8192,1,1024]{3,2,1,0:T(1,128)} %win_ref.7), custom_call_target="tpu_custom_call" | custom-call | tf_op jit(solution)/shard_map/pack/pallas_call | solution.py:55
  9.7 2.4 %pack.4.refs_0_ = f32[1024,128]{1,0:T(8,128)S(1)} custom-call(f32[1,8192,1,1024]{3,2,1,0:T(1,128)} %win_ref.7), custom_call_target="tpu_custom_call" | custom-call | tf_op jit(solution)/shard_map/pack/pallas_call | solution.py:55
  12.1 1.0 collective-permute-done.4.refs_1_
  14.5 1.2 collective-permute-start.3
  15.7 1.0 collective-permute-done.8
  17.6 1.5 collective-permute-start.9
  19.1 5.6 %collective-permute-start = (f32[2304,128]{1,0:T(8,128)S(1)}, f32[2304,128]{1,0:T(8,128)}, u32[]{:S(2)}, u32[]{:S(2)}) collective-permute-start(f32[2304,128]{1,0:T(8,128)S(1)} %pack.6.refs_0_), channel_id=1, source_target_pairs={{0,1},{1,2},{2,3},{4,5},{5,6},{6,7},{8,9},{9,10},{10,11},{12,13},{... | collective-permute-start | bytes 3538952 | tf_op jit(solution)/shard_map/ppermute | solution.py:415
  24.7 1.9 %collective-permute-start.1 = (f32[2304,128]{1,0:T(8,128)S(1)}, f32[2304,128]{1,0:T(8,128)}, u32[]{:S(2)}, u32[]{:S(2)}) collective-permute-start(f32[2304,128]{1,0:T(8,128)S(1)} %pack.6.refs_0_), channel_id=1, source_target_pairs={{1,0},{2,1},{3,2},{5,4},{6,5},{7,6},{9,8},{10,9},{11,10},{13,12},{... | collective-permute-start | bytes 3538952 | tf_op jit(solution)/shard_map/ppermute | solution.py:415
  27.7 9.5 %all_gather.3.s_ref = f32[8,32,256]{2,1,0:T(8,128)S(1)} all-gather(f32[1,32,256]{2,1,0:T(8,128)S(1)} %all_gather_reshape.3), channel_id=1, replica_groups=mesh['row'=8,'col'=4] {'row'}, dimensions={0}, use_global_device_ids=true | all-gather | bytes 294912 | tf_op jit(solution)/shard_map/all_gather | solution.py:373
  37.2 27.8 %factor.1 = (bf16[256,256]{1,0:T(8,128)(2,1)S(1)}, bf16[256,256]{1,0:T(8,128)(2,1)S(1)}, f32[32,256]{1,0:T(8,128)S(1)}) custom-call(s32[2]{0:T(128)S(1)} %pad_add_fusion.place_ref, f32[8,32,256]{2,1,0:T(8,128)S(1)} %all_gather.3.s_ref), custom_call_target="tpu_custom_call" | custom-call | tf_op jit(solution)/shard_map/factor/pallas_call | solution.py:159
  65.0 2.4 %collective-permute-done.3.refs_2_ = f32[2304,128]{1,0:T(8,128)S(1)} collective-permute-done((f32[2304,128]{1,0:T(8,128)S(1)}, f32[2304,128]{1,0:T(8,128)S(1)}, u32[]{:S(2)}, u32[]{:S(2)}) %collective-permute-start.3) | collective-permute-done | bytes 1179680 | tf_op jit(solution)/shard_map/ppermute | solution.py:363
  67.3 6.2 %collective-permute-start.7 = (f32[2304,128]{1,0:T(8,128)S(1)}, f32[2304,128]{1,0:T(8,128)}, u32[]{:S(2)}, u32[]{:S(2)}) collective-permute-start(f32[2304,128]{1,0:T(8,128)S(1)} %collective-permute-done.3.refs_2_), channel_id=1, source_target_pairs={{2,3},{1,0},{6,7},{5,4},{10,11},{9,8},{14,15},{13,12},{18,19},{17,... | collective-permute-start | bytes 3538952 | tf_op jit(solution)/shard_map/ppermute | solution.py:415
  73.5 1.9 %select_bitcast_fusion = f32[1,4,256,128]{3,2,1,0:T(8,128)} fusion(f32[4,256,128]{2,1,0:T(8,128)} %collective-permute-done.9, pred[]{:T(512)S(6)} %ne.6, f32[4,256,128]{2,1,0:T(8,128)} %collective-permute-done.8, f32[1,256,128]{2,1,0:T(8,128)} %bitcast.27, f32[1,256,128]{2,1,0:T(8,128)S(1)} %bitcast.24, f32[1,256,128]{2,1,0:T(8,128)S(1)} %bitcast.21, ...), kind=kLoop, calls=%fused_computation.2 | loop fusion | flops 655360 | bytes 2097154 | tf_op jit(solution)/shard_map/broadcast_in_dim | solution.py:383
  75.4 1.5 collective-permute-start.10
  77.0 1.2 pack.5.refs_0_
  78.9 15.5 %collective-permute-done.refs_1_ = f32[2304,128]{1,0:T(8,128)} collective-permute-done((f32[2304,128]{1,0:T(8,128)S(1)}, f32[2304,128]{1,0:T(8,128)}, u32[]{:S(2)}, u32[]{:S(2)}) %collective-permute-start) | collective-permute-done | bytes 1179680 | tf_op jit(solution)/shard_map/ppermute | solution.py:415
  94.5 3.7 %collective-permute-start.15 = (f32[1024,128]{1,0:T(8,128)S(1)}, f32[1024,128]{1,0:T(8,128)S(1)}, u32[]{:S(2)}, u32[]{:S(2)}) collective-permute-start(f32[1024,128]{1,0:T(8,128)S(1)} %pack.4.refs_0_), channel_id=1, source_target_pairs={{0,1},{1,2},{2,3},{4,5},{5,6},{6,7},{8,9},{9,10},{10,11},{12,13},{... | collective-permute-start | bytes 1572872 | tf_op jit(solution)/shard_map/ppermute | solution.py:415
  98.2 2.3 %collective-permute-start.16 = (f32[1024,128]{1,0:T(8,128)S(1)}, f32[1024,128]{1,0:T(8,128)S(1)}, u32[]{:S(2)}, u32[]{:S(2)}) collective-permute-start(f32[1024,128]{1,0:T(8,128)S(1)} %pack.4.refs_0_), channel_id=1, source_target_pairs={{1,0},{2,1},{3,2},{5,4},{6,5},{7,6},{9,8},{10,9},{11,10},{13,12},{... | collective-permute-start | bytes 1572872 | tf_op jit(solution)/shard_map/ppermute | solution.py:415
  100.5 1.3 broadcast_select_fusion.2
  101.9 1.5 columns.1
  105.1 5.2 %update.5.refs_11_ = f32[65536,128]{1,0:T(8,128)} custom-call(s32[2]{0:T(128)S(1)} %pad_add_fusion.place_ref, f32[256,128]{1,0:T(8,128)S(1)} %pack.7.refs_0_, f32[256,128]{1,0:T(8,128)S(1)} %collective-permute-done.4.refs_1_, f32[256,128]{1,0:T(8,128)S(1)} %collective-permute-done.5.refs_2_, f32[256,128]{1,0:T(8,128)S(1)} %copy-done.1, ...), custom_call_target="tpu_custom_call" | custom-call | flops 1006632960 | bytes 4718592 | tf_op jit(solution)/shard_map/update/pallas_call | solution.py:311
  110.3 13.8 %update.6.refs_11_ = f32[65536,128]{1,0:T(8,128)} custom-call(s32[2]{0:T(128)S(1)} %pad_add_fusion.place_ref, f32[2304,128]{1,0:T(8,128)S(1)} %pack.6.refs_0_, f32[2304,128]{1,0:T(8,128)} %collective-permute-done.refs_1_, f32[2304,128]{1,0:T(8,128)S(1)} %collective-permute-done.3.refs_2_, ...), custom_call_target="tpu_custom_call", output_to_operand_aliasing={{}: (12, {})} | custom-call | flops 5033164800 | bytes 23592960 | tf_op jit(solution)/shard_map/update/pallas_call | solution.py:311
  124.1 3.8 %collective-permute-start.17 = (f32[1024,128]{1,0:T(8,128)S(1)}, f32[1024,128]{1,0:T(8,128)S(1)}, u32[]{:S(2)}, u32[]{:S(2)}) collective-permute-start(f32[1024,128]{1,0:T(8,128)S(1)} %collective-permute-done.2.refs_2_), channel_id=1, source_target_pairs={{2,3},{1,0},{6,7},{5,4},{10,11},{9,8},{14,15},{13,12},{18,19},{17,... | collective-permute-start | bytes 1572872 | tf_op jit(solution)/shard_map/ppermute | solution.py:415
  127.9 1.9 %collective-permute-start.11 = (f32[512,128]{1,0:T(8,128)S(1)}, f32[512,128]{1,0:T(8,128)S(1)}, u32[]{:S(2)}, u32[]{:S(2)}) collective-permute-start(f32[512,128]{1,0:T(8,128)S(1)} %copy-done.3), channel_id=1, source_target_pairs={{0,1},{1,2},{2,3},{4,5},{5,6},{6,7},{8,9},{9,10},{10,11},{12,13},{... | collective-permute-start | bytes 786440 | tf_op jit(solution)/shard_map/ppermute | solution.py:415
  129.9 12.0 %update.7.refs_11_ = f32[65536,128]{1,0:T(8,128)} custom-call(s32[2]{0:T(128)S(1)} %pad_add_fusion.place_ref, f32[2304,128]{1,0:T(8,128)S(1)} %pack.6.refs_0_, f32[2304,128]{1,0:T(8,128)} %collective-permute-done.refs_1_, f32[2304,128]{1,0:T(8,128)S(1)} %collective-permute-done.3.refs_2_, ...), custom_call_target="tpu_custom_call", output_to_operand_aliasing={{}: (12, {})} | custom-call | flops 4026531840 | bytes 18874368 | tf_op jit(solution)/shard_map/update/pallas_call | solution.py:311
  141.9 3.9 %collective-permute-start.13 = (f32[512,128]{1,0:T(8,128)S(1)}, f32[512,128]{1,0:T(8,128)S(1)}, u32[]{:S(2)}, u32[]{:S(2)}) collective-permute-start(f32[512,128]{1,0:T(8,128)S(1)} %copy-done.3), channel_id=1, source_target_pairs={{1,0},{2,1},{3,2},{5,4},{6,5},{7,6},{9,8},{10,9},{11,10},{13,12},{... | collective-permute-start | bytes 786440 | tf_op jit(solution)/shard_map/ppermute | solution.py:415
  145.9 2.0 %collective-permute-start.14 = (f32[512,128]{1,0:T(8,128)S(1)}, f32[512,128]{1,0:T(8,128)S(1)}, u32[]{:S(2)}, u32[]{:S(2)}) collective-permute-start(f32[512,128]{1,0:T(8,128)S(1)} %collective-permute-done.12.refs_2_), channel_id=1, source_target_pairs={{2,3},{1,0},{6,7},{5,4},{10,11},{9,8},{14,15},{13,12},{18,19},{17,... | collective-permute-start | bytes 786440 | tf_op jit(solution)/shard_map/ppermute | solution.py:415
  147.8 10.1 %update.8.refs_11_ = f32[65536,128]{1,0:T(8,128)} custom-call(s32[2]{0:T(128)S(1)} %pad_add_fusion.place_ref, f32[1024,128]{1,0:T(8,128)S(1)} %pack.4.refs_0_, f32[1024,128]{1,0:T(8,128)S(1)} %collective-permute-done.15.refs_1_, f32[1024,128]{1,0:T(8,128)S(1)} %collective-permute-done.2.refs_2_, ...), custom_call_target="tpu_custom_call", output_to_operand_aliasing={{}: (12, {})} | custom-call | flops 4026531840 | bytes 18874368 | tf_op jit(solution)/shard_map/update/pallas_call | solution.py:311
  157.9 6.5 %update.9 = f32[65536,128]{1,0:T(8,128)} custom-call(s32[2]{0:T(128)S(1)} %pad_add_fusion.place_ref, f32[512,128]{1,0:T(8,128)S(1)} %copy-done.3, f32[512,128]{1,0:T(8,128)S(1)} %collective-permute-done.11.refs_1_, f32[512,128]{1,0:T(8,128)S(1)} %collective-permute-done.12.refs_2_, ...), custom_call_target="tpu_custom_call", output_to_operand_aliasing={{}: (12, {})} | custom-call | flops 2013265920 | bytes 9437184 | tf_op jit(solution)/shard_map/update/pallas_call | solution.py:311
  (39 shorter events, 6.1 us)
Async XLA Ops:
  1.1 12.1 %collective-permute-start.4 = (f32[256,128]{1,0:T(8,128)S(1)}, f32[256,128]{1,0:T(8,128)S(1)}, u32[]{:S(2)}, u32[]{:S(2)}) collective-permute-start(f32[256,128]{1,0:T(8,128)S(1)} %pack.7.refs_0_), channel_id=1, source_target_pairs={{0,1},{1,2},{2,3},{3,0},{4,5},{5,6},{6,7},{7,4},{8,9},{9,10},{10,1... | collective-permute-start | bytes 393224 | tf_op jit(solution)/shard_map/ppermute | solution.py:363
  2.7 10.4 %collective-permute-start.5 = (f32[256,128]{1,0:T(8,128)S(1)}, f32[256,128]{1,0:T(8,128)S(1)}, u32[]{:S(2)}, u32[]{:S(2)}) collective-permute-start(f32[256,128]{1,0:T(8,128)S(1)} %pack.7.refs_0_), channel_id=1, source_target_pairs={{0,2},{1,3},{2,0},{3,1},{4,6},{5,7},{6,4},{7,5},{8,10},{9,11},{10,... | collective-permute-start | bytes 393224 | tf_op jit(solution)/shard_map/ppermute | solution.py:363
  3.0 10.6 %collective-permute-start.6 = (f32[256,128]{1,0:T(8,128)S(1)}, f32[256,128]{1,0:T(8,128)S(1)}, u32[]{:S(2)}, u32[]{:S(2)}) collective-permute-start(f32[256,128]{1,0:T(8,128)S(1)} %pack.7.refs_0_), channel_id=1, source_target_pairs={{0,3},{1,0},{2,1},{3,2},{4,7},{5,4},{6,5},{7,6},{8,11},{9,8},{10,9... | collective-permute-start | bytes 393224 | tf_op jit(solution)/shard_map/ppermute | solution.py:363
  13.6 14.0 %copy-start = (f32[256,128]{1,0:T(8,128)}, f32[256,128]{1,0:T(8,128)S(1)}, u32[]{:S(2)}) copy-start(f32[256,128]{1,0:T(8,128)S(1)} %collective-permute-done.6.refs_3_) | copy-start | bytes 393220
  14.5 2.3 %collective-permute-start.8 = (f32[4,256,128]{2,1,0:T(8,128)}, f32[4,256,128]{2,1,0:T(8,128)}, u32[]{:S(2)}, u32[]{:S(2)}) collective-permute-start(f32[4,256,128]{2,1,0:T(8,128)} %pad_maximum_fusion), channel_id=1, source_target_pairs={{0,4},{4,0},{8,12},{12,8},{16,20},{20,16},{24,28},{28,24},{1,5},{5... | collective-permute-start | bytes 1572872 | tf_op jit(solution)/shard_map/ppermute | solution.py:380
  14.5 52.8 %collective-permute-start.3 = (f32[2304,128]{1,0:T(8,128)S(1)}, f32[2304,128]{1,0:T(8,128)S(1)}, u32[]{:S(2)}, u32[]{:S(2)}) collective-permute-start(f32[2304,128]{1,0:T(8,128)S(1)} %pack.6.refs_0_), channel_id=1, source_target_pairs={{0,2},{1,3},{2,0},{3,1},{4,6},{5,7},{6,4},{7,5},{8,10},{9,11},{10,... | collective-permute-start | bytes 3538952 | tf_op jit(solution)/shard_map/ppermute | solution.py:363
  17.6 55.9 %collective-permute-start.9 = (f32[4,256,128]{2,1,0:T(8,128)}, f32[4,256,128]{2,1,0:T(8,128)}, u32[]{:S(2)}, u32[]{:S(2)}) collective-permute-start(f32[4,256,128]{2,1,0:T(8,128)} %broadcast_select_fusion), channel_id=1, source_target_pairs={{0,8},{4,12},{8,0},{12,4},{16,24},{20,28},{24,16},{28,20},{1,9},{5... | collective-permute-start | bytes 1572872 | tf_op jit(solution)/shard_map/ppermute | solution.py:380
  19.1 75.4 %collective-permute-start = (f32[2304,128]{1,0:T(8,128)S(1)}, f32[2304,128]{1,0:T(8,128)}, u32[]{:S(2)}, u32[]{:S(2)}) collective-permute-start(f32[2304,128]{1,0:T(8,128)S(1)} %pack.6.refs_0_), channel_id=1, source_target_pairs={{0,1},{1,2},{2,3},{4,5},{5,6},{6,7},{8,9},{9,10},{10,11},{12,13},{... | collective-permute-start | bytes 3538952 | tf_op jit(solution)/shard_map/ppermute | solution.py:415
  24.7 69.8 %collective-permute-start.1 = (f32[2304,128]{1,0:T(8,128)S(1)}, f32[2304,128]{1,0:T(8,128)}, u32[]{:S(2)}, u32[]{:S(2)}) collective-permute-start(f32[2304,128]{1,0:T(8,128)S(1)} %pack.6.refs_0_), channel_id=1, source_target_pairs={{1,0},{2,1},{3,2},{5,4},{6,5},{7,6},{9,8},{10,9},{11,10},{13,12},{... | collective-permute-start | bytes 3538952 | tf_op jit(solution)/shard_map/ppermute | solution.py:415
  64.9 10.5 %copy-start.4 = (f32[32,256]{1,0:T(8,128)}, f32[32,256]{1,0:T(8,128)S(1)}, u32[]{:S(2)}) copy-start(f32[32,256]{1,0:T(8,128)S(1)} %get-tuple-element.37.refs_8_.refs_9_) | copy-start | bytes 98308
  67.3 42.9 %collective-permute-start.7 = (f32[2304,128]{1,0:T(8,128)S(1)}, f32[2304,128]{1,0:T(8,128)}, u32[]{:S(2)}, u32[]{:S(2)}) collective-permute-start(f32[2304,128]{1,0:T(8,128)S(1)} %collective-permute-done.3.refs_2_), channel_id=1, source_target_pairs={{2,3},{1,0},{6,7},{5,4},{10,11},{9,8},{14,15},{13,12},{18,19},{17,... | collective-permute-start | bytes 3538952 | tf_op jit(solution)/shard_map/ppermute | solution.py:415
  75.4 25.0 %collective-permute-start.10 = (f32[1,4,256,128]{3,2,1,0:T(8,128)}, f32[1,4,256,128]{3,2,1,0:T(8,128)}, u32[]{:S(2)}, u32[]{:S(2)}) collective-permute-start(f32[1,4,256,128]{3,2,1,0:T(8,128)} %select_bitcast_fusion), channel_id=1, source_target_pairs={{0,16},{4,20},{8,24},{12,28},{16,0},{20,4},{24,8},{28,12},{1,17},{... | collective-permute-start | bytes 1572872 | tf_op jit(solution)/shard_map/ppermute | solution.py:386
  78.2 0.7 copy-start.2
  94.5 29.6 %collective-permute-start.2 = (f32[1024,128]{1,0:T(8,128)S(1)}, f32[1024,128]{1,0:T(8,128)S(1)}, u32[]{:S(2)}, u32[]{:S(2)}) collective-permute-start(f32[1024,128]{1,0:T(8,128)S(1)} %pack.4.refs_0_), channel_id=1, source_target_pairs={{0,2},{1,3},{2,0},{3,1},{4,6},{5,7},{6,4},{7,5},{8,10},{9,11},{10,... | collective-permute-start | bytes 1572872 | tf_op jit(solution)/shard_map/ppermute | solution.py:363
  94.5 51.4 %collective-permute-start.15 = (f32[1024,128]{1,0:T(8,128)S(1)}, f32[1024,128]{1,0:T(8,128)S(1)}, u32[]{:S(2)}, u32[]{:S(2)}) collective-permute-start(f32[1024,128]{1,0:T(8,128)S(1)} %pack.4.refs_0_), channel_id=1, source_target_pairs={{0,1},{1,2},{2,3},{4,5},{5,6},{6,7},{8,9},{9,10},{10,11},{12,13},{... | collective-permute-start | bytes 1572872 | tf_op jit(solution)/shard_map/ppermute | solution.py:415
  98.2 49.7 %collective-permute-start.16 = (f32[1024,128]{1,0:T(8,128)S(1)}, f32[1024,128]{1,0:T(8,128)S(1)}, u32[]{:S(2)}, u32[]{:S(2)}) collective-permute-start(f32[1024,128]{1,0:T(8,128)S(1)} %pack.4.refs_0_), channel_id=1, source_target_pairs={{1,0},{2,1},{3,2},{5,4},{6,5},{7,6},{9,8},{10,9},{11,10},{13,12},{... | collective-permute-start | bytes 1572872 | tf_op jit(solution)/shard_map/ppermute | solution.py:415
  103.4 0.9 copy-start.1
  104.3 0.8 copy-start.5
  105.1 5.2 %copy-start.6 = (f32[32,256]{1,0:T(8,128)S(1)}, f32[32,256]{1,0:T(8,128)}, u32[]{:S(2)}) copy-start(f32[32,256]{1,0:T(8,128)} %copy-done.4) | copy-start | bytes 98308
  110.2 17.6 %copy-start.3 = (f32[512,128]{1,0:T(8,128)S(1)}, f32[512,128]{1,0:T(8,128)}, u32[]{:S(2)}) copy-start(f32[512,128]{1,0:T(8,128)} %copy-done.2) | copy-start | bytes 786436
  124.1 23.8 %collective-permute-start.17 = (f32[1024,128]{1,0:T(8,128)S(1)}, f32[1024,128]{1,0:T(8,128)S(1)}, u32[]{:S(2)}, u32[]{:S(2)}) collective-permute-start(f32[1024,128]{1,0:T(8,128)S(1)} %collective-permute-done.2.refs_2_), channel_id=1, source_target_pairs={{2,3},{1,0},{6,7},{5,4},{10,11},{9,8},{14,15},{13,12},{18,19},{17,... | collective-permute-start | bytes 1572872 | tf_op jit(solution)/shard_map/ppermute | solution.py:415
  127.9 14.1 %collective-permute-start.12 = (f32[512,128]{1,0:T(8,128)S(1)}, f32[512,128]{1,0:T(8,128)S(1)}, u32[]{:S(2)}, u32[]{:S(2)}) collective-permute-start(f32[512,128]{1,0:T(8,128)S(1)} %copy-done.3), channel_id=1, source_target_pairs={{0,2},{1,3},{2,0},{3,1},{4,6},{5,7},{6,4},{7,5},{8,10},{9,11},{10,... | collective-permute-start | bytes 786440 | tf_op jit(solution)/shard_map/ppermute | solution.py:363
  127.9 30.0 %collective-permute-start.11 = (f32[512,128]{1,0:T(8,128)S(1)}, f32[512,128]{1,0:T(8,128)S(1)}, u32[]{:S(2)}, u32[]{:S(2)}) collective-permute-start(f32[512,128]{1,0:T(8,128)S(1)} %copy-done.3), channel_id=1, source_target_pairs={{0,1},{1,2},{2,3},{4,5},{5,6},{6,7},{8,9},{9,10},{10,11},{12,13},{... | collective-permute-start | bytes 786440 | tf_op jit(solution)/shard_map/ppermute | solution.py:415
  141.9 16.0 %collective-permute-start.13 = (f32[512,128]{1,0:T(8,128)S(1)}, f32[512,128]{1,0:T(8,128)S(1)}, u32[]{:S(2)}, u32[]{:S(2)}) collective-permute-start(f32[512,128]{1,0:T(8,128)S(1)} %copy-done.3), channel_id=1, source_target_pairs={{1,0},{2,1},{3,2},{5,4},{6,5},{7,6},{9,8},{10,9},{11,10},{13,12},{... | collective-permute-start | bytes 786440 | tf_op jit(solution)/shard_map/ppermute | solution.py:415
  145.9 12.1 %collective-permute-start.14 = (f32[512,128]{1,0:T(8,128)S(1)}, f32[512,128]{1,0:T(8,128)S(1)}, u32[]{:S(2)}, u32[]{:S(2)}) collective-permute-start(f32[512,128]{1,0:T(8,128)S(1)} %collective-permute-done.12.refs_2_), channel_id=1, source_target_pairs={{2,3},{1,0},{6,7},{5,4},{10,11},{9,8},{14,15},{13,12},{18,19},{17,... | collective-permute-start | bytes 786440 | tf_op jit(solution)/shard_map/ppermute | solution.py:415
